TPU v7x, 256 devices: a whole 4x4x8 slice. The times are simulated.
256 devices in a mesh: user: 16 (over y, x), track: 16 (over z, core).
Axes of the slice: x: 4, y: 4, z: 8, core: 2. Of those that a mesh axis runs over, the one named last changes fastest.
Arguments:
- user_emb: float32 [32768, 128], P(('user', 'track')), may hold values from -6 to 6
- user_cot: float32 [32768, 128], P(('user', 'track')), may hold values from -6 to 6
- track_emb: float32 [32768, 128], P('track'), may hold values from -6 to 6
- track_cot: float32 [32768, 128], P('track'), may hold values from -6 to 6
- user_degree: int32 [32768], P(('user', 'track')), may hold values from 32768 to 131071
- track_degree: int32 [32768], P('track'), may hold values from 32768 to 131071
- tile_vals: float32 [16, 16, 128, 128, 128], P('user', 'track'), may hold values from 0 to 512
- tile_rows: int32 [16, 16, 128], P('user', 'track'), may hold values from 0 to 15
- tile_cols: int32 [16, 16, 128], P('user', 'track'), may hold values from 0 to 15
- tile_count: int32 [16, 16], P('user', 'track'), may hold values from 12 to 128, as said below
Outputs:
- user_out: float32 [32768, 128], P(('user', 'track'))
- user_grad: float32 [32768, 128], P(('user', 'track'))
- track_out: float32 [16, 16, 128, 128], P('user', 'track')
- track_grad: float32 [16, 16, 128, 128], P('user', 'track')
Inputs may be any that keep to these rules, and one draw needn't show every extreme that they name: Only the first tile_count[a, b] slots of grid cell (a, b) hold tiles; some cell is full in every draw. Live slots may repeat a tile position, and then their tiles add.
All inputs are finite; a program needn't handle non-finite values.
Results may differ from a plain program's by a relative error of at most 0.0003.
Values sent between devices are 32-bit elements; how exact they have to be, the bound alone decides.
No kernel may reach another device: no remote copies, remote signals or barrier semaphores. Data moves between devices by JAX's collectives and lax.ppermute only.
A program may use at most 128 MiB of HBM per device.

v0:
```python
import jax
import jax.numpy as jnp
from jax import lax
from jax.sharding import PartitionSpec as P


def body(
    user_emb,
    user_cot,
    track_emb,
    track_cot,
    user_degree,
    track_degree,
    tile_vals,
    tile_rows,
    tile_cols,
    tile_count,
):
    highest = lax.Precision.HIGHEST
    user_ways = lax.axis_size("user")
    track_ways = lax.axis_size("track")
    emb_width = user_emb.shape[1]
    tile_size = tile_vals.shape[-1]
    slot_total = tile_vals.shape[2]
    col_tiles = track_emb.shape[0] // tile_size
    row_tiles = user_emb.shape[0] * track_ways // tile_size
    user_scale = 1.0 / jnp.sqrt(user_degree.astype(jnp.float32))
    track_scale = 1.0 / jnp.sqrt(track_degree.astype(jnp.float32))
    user_piece = jnp.concatenate([user_emb, user_cot], axis=1) * user_scale[:, None]
    track_block = jnp.concatenate([track_emb, track_cot], axis=1) * track_scale[:, None]
    groups = col_tiles // track_ways
    moving = track_block.reshape(groups, track_ways, tile_size, 2 * emb_width)
    moving_scale = track_scale.reshape(groups, track_ways, tile_size)
    arrived, arrived_scale = (
        lax.all_to_all(moving, "track", split_axis=1, concat_axis=0, tiled=True),
        lax.all_to_all(moving_scale, "track", split_axis=1, concat_axis=0, tiled=True),
    )
    track_panel = arrived.reshape(col_tiles, tile_size, 2 * emb_width)
    cyclic_scale = arrived_scale.reshape(col_tiles, tile_size)
    user_panel = lax.all_gather(user_piece, "track", axis=0, tiled=True).reshape(
        row_tiles, tile_size, 2 * emb_width
    )
    values = tile_vals.reshape(slot_total, tile_size, tile_size)
    row_ids = tile_rows.reshape(slot_total)
    col_ids = tile_cols.reshape(slot_total)
    live_count = tile_count.reshape(())
    step_slots = min(32, slot_total)
    user_flat = user_panel.reshape(row_tiles, tile_size * 2 * emb_width)
    track_flat = track_panel.reshape(col_tiles, tile_size * 2 * emb_width)

    def one_block(block_index, block_sums):
        user_acc, track_acc = block_sums
        first_slot = block_index * step_slots
        block_values = lax.dynamic_slice_in_dim(values, first_slot, step_slots, 0)
        block_rows = lax.dynamic_slice_in_dim(row_ids, first_slot, step_slots, 0)
        block_cols = lax.dynamic_slice_in_dim(col_ids, first_slot, step_slots, 0)
        live_mask = (first_slot + jnp.arange(step_slots, dtype=jnp.int32) < live_count).astype(
            jnp.float32
        )
        block_values = block_values * live_mask[:, None, None]
        row_pick = (block_rows[:, None] == jnp.arange(row_tiles, dtype=jnp.int32)[None, :]).astype(
            jnp.float32
        )
        col_pick = (block_cols[:, None] == jnp.arange(col_tiles, dtype=jnp.int32)[None, :]).astype(
            jnp.float32
        )
        from_tracks = jnp.dot(col_pick, track_flat, precision=highest).reshape(
            step_slots, tile_size, 2 * emb_width
        )
        from_users = jnp.dot(row_pick, user_flat, precision=highest).reshape(
            step_slots, tile_size, 2 * emb_width
        )
        to_users = jnp.einsum("kij,kje->kie", block_values, from_tracks, precision=highest).reshape(
            step_slots, -1
        )
        to_tracks = jnp.einsum("kij,kie->kje", block_values, from_users, precision=highest).reshape(
            step_slots, -1
        )
        user_acc = user_acc + jnp.dot(row_pick.T, to_users, precision=highest)
        track_acc = track_acc + jnp.dot(col_pick.T, to_tracks, precision=highest)
        return (user_acc, track_acc)

    blocks_live = (live_count + step_slots - 1) // step_slots
    start_sums = (jnp.zeros_like(user_flat), jnp.zeros_like(track_flat))
    user_acc, track_acc = lax.fori_loop(0, blocks_live, one_block, start_sums)
    user_sums = user_acc.reshape(row_tiles * tile_size, 2 * emb_width)
    track_sums = track_acc.reshape(col_tiles, tile_size, 2 * emb_width)
    user_total = (
        lax.psum_scatter(user_sums, "track", scatter_dimension=0, tiled=True) * user_scale[:, None]
    )
    track_total = lax.psum_scatter(track_sums, "user", scatter_dimension=0, tiled=True)
    own_tiles = col_tiles // user_ways
    own_scale = lax.dynamic_slice_in_dim(
        cyclic_scale, lax.axis_index("user") * own_tiles, own_tiles, 0
    )
    track_total = (track_total * own_scale[:, :, None]).reshape(
        own_tiles, 1, tile_size, 2 * emb_width
    )
    return (
        user_total[:, :emb_width],
        user_total[:, emb_width:],
        track_total[..., :emb_width],
        track_total[..., emb_width:],
    )


def solution(mesh):
    placed = (
        P(("user", "track"), None),
        P(("user", "track"), None),
        P("track", None),
        P("track", None),
        P(("user", "track")),
        P("track"),
        P("user", "track", None, None, None),
        P("user", "track", None),
        P("user", "track", None),
        P("user", "track"),
    )
    return jax.shard_map(
        body,
        mesh=mesh,
        in_specs=placed,
        out_specs=(
            P(("user", "track"), None),
            P(("user", "track"), None),
            P("user", "track", None, None),
            P("user", "track", None, None),
        ),
        check_vma=False,
    )
```

profile of v0, /device:TPU:1, one launch (start us, length us, event | category | flops | bytes accessed | tf_op | source)
XLA Modules:
  0.0 358.3 jit_solution(13780315538488632619)
XLA Ops:
  8.5 3.3 maximum_multiply_fusion
  11.8 10.1 %all-to-all-start = ((f32[1,16,128,256]{3,2,0,1:T(8,128)}), f32[1,16,128,256]{3,2,0,1:T(8,128)S(1)}, u32[]{:S(2)}, u32[]{:S(2)}) async-start(f32[1,16,128,256]{3,2,0,1:T(8,128)} %maximum_multiply_fusion), calls=%async_computation | async-start | bytes 4194304 | tf_op jit(solution)/shard_map/all_to_all | solution.py:35
  23.4 9.1 %copy.17 = f32[1,1,128,128,128]{3,4,2,1,0:T(8,128)} copy(f32[1,1,128,128,128]{4,3,2,1,0:T(8,128)} %param.18) | data formatting | bytes 16777216 | tf_op args[6]
  32.5 46.5 %all-to-all-done = f32[1,16,128,256]{3,2,0,1:T(8,128)S(1)} async-done(((f32[1,16,128,256]{3,2,0,1:T(8,128)}), f32[1,16,128,256]{3,2,0,1:T(8,128)S(1)}, u32[]{:S(2)}, u32[]{:S(2)}) %all-to-all-start) | async-done | bytes 2097184 | tf_op jit(solution)/shard_map/all_to_all | solution.py:35
  79.0 2.6 copy.23
  81.6 2.8 all-gather.2.cloned.1.call-done
  84.4 2.7 reshape_reshape.7
  87.2 1.5 broadcast.25
  88.7 30.5 %while.12 = (s32[]{:T(128)}, f32[16,32768]{1,0:T(8,128)}, f32[16,32768]{1,0:T(8,128)S(1)}, s32[]{:T(128)}, s32[128]{0:T(128)S(1)}, /*index=5*/f32[128,128,128]{1...) while((s32[]{:T(128)}, f32[16,32768]{1,0:T(8,128)}, ...), condition=%wide.region_1.2_spmd, body=%wide.region_0.1_spmd.sunk | while | flops 4028631040 | bytes 142608832 | solution.py:85
  89.5 3.4 fusion.39
  94.3 2.1 copy-done
  96.4 3.9 %fusion.40 = f32[32,128,256]{2,1,0:T(8,128)S(1)} fusion(f32[32,128,256]{2,1,0:T(8,128)S(1)} %bitcast.67, f32[128,128,128]{1,2,0:T(8,128)S(1)} %copy-done, s32[]{:T(128)S(6)} %select_n.16, f32[32]{0:T(128)S(1)} %compare_convert_fusion.2), kind=kOutput, calls=%fused_computation.3.clone.1 | convolution fusion | flops 1611137024 | bytes 10486276 | tf_op jit(solution)/shard_map/while/body/kij,kie->kje/dot_general | solution.py:76
  100.3 2.4 copy.32
  102.8 2.8 convolution_add_fusion.5
  105.6 1.8 fusion.37
  108.7 4.0 %fusion.38 = f32[32,128,256]{2,1,0:T(8,128)S(1)} fusion(f32[32,128,256]{2,1,0:T(8,128)S(1)} %bitcast.63, f32[128,128,128]{1,2,0:T(8,128)S(1)} %copy-done, s32[]{:T(128)S(6)} %select_n.16, f32[32]{0:T(128)S(1)} %compare_convert_fusion.2), kind=kOutput, calls=%fused_computation.4.clone.1 | convolution fusion | flops 1611137024 | bytes 10486276 | tf_op jit(solution)/shard_map/while/body/kij,kje->kie/dot_general | solution.py:73
  112.7 2.4 copy.30
  115.1 2.8 convolution_add_fusion.4
  119.3 2.0 copy.24
  121.3 1.5 copy-done.3
  124.3 98.6 %all-to-all-start.1 = ((f32[1,16,128]{2,0,1:T(1,128)}), f32[1,16,128]{2,0,1:T(1,128)S(1)}, u32[]{:S(2)}, u32[]{:S(2)}) async-start(f32[1,16,128]{2,0,1:T(1,128)} %bitcast.7), calls=%async_computation.2 | async-start | bytes 16384 | tf_op jit(solution)/shard_map/all_to_all | solution.py:36
  222.9 6.9 %all-to-all-done.1 = f32[1,16,128]{2,0,1:T(1,128)S(1)} async-done(((f32[1,16,128]{2,0,1:T(1,128)}), f32[1,16,128]{2,0,1:T(1,128)S(1)}, u32[]{:S(2)}, u32[]{:S(2)}) %all-to-all-start.1) | async-done | bytes 8224 | tf_op jit(solution)/shard_map/all_to_all | solution.py:36
  229.9 60.2 %reduce-scatter.7.cloned.1.call-done = f32[1,128,256]{2,1,0:T(8,128)} async-done(((f32[16,128,256]{2,1,0:T(8,128)}), f32[1,128,256]{2,1,0:T(8,128)}) %reduce-scatter.7.cloned.1.call-update) | async-done | bytes 131088
  291.7 58.4 %reduce-scatter.5.cloned.1.call-done = f32[128,256]{1,0:T(8,128)} async-done(((f32[2048,256]{1,0:T(8,128)}), f32[128,256]{1,0:T(8,128)}) %reduce-scatter.5.cloned.1.call-update) | async-done | bytes 131088 | tf_op jit(solution)/shard_map/reduce_scatter | solution.py:89
  (39 shorter events, 11.8 us)
Async XLA Ops:
  11.8 10.2 %copy-start.7 = (s32[128]{0:T(128)S(1)}, s32[128]{0:T(128)}, u32[]{:S(2)}) copy-start(s32[128]{0:T(128)} %param.16) | copy-start | bytes 1540
  11.8 10.2 %copy-start.5 = (f32[128,128]{1,0:T(8,128)S(1)}, f32[128,128]{1,0:T(8,128)}, u32[]{:S(2)}) copy-start(f32[128,128]{1,0:T(8,128)} %param.13) | copy-start | bytes 196612
  11.8 10.2 %copy-start.6 = (f32[128,128]{1,0:T(8,128)S(1)}, f32[128,128]{1,0:T(8,128)}, u32[]{:S(2)}) copy-start(f32[128,128]{1,0:T(8,128)} %param.12) | copy-start | bytes 196612
  11.8 67.2 %all-to-all-start = ((f32[1,16,128,256]{3,2,0,1:T(8,128)}), f32[1,16,128,256]{3,2,0,1:T(8,128)S(1)}, u32[]{:S(2)}, u32[]{:S(2)}) async-start(f32[1,16,128,256]{3,2,0,1:T(8,128)} %maximum_multiply_fusion), calls=%async_computation | async-start | bytes 4194304 | tf_op jit(solution)/shard_map/all_to_all | solution.py:35
  21.9 62.5 %all-gather.2.cloned.1.call-start = ((), (), s32[]{:S(2)}) async-start(), calls=%async_computation.4 | async-start | bytes 2228224 | tf_op jit(solution)/shard_map/all_gather | solution.py:40
  22.7 267.3 %reduce-scatter.7.cloned.1.call-start = ((), (), s32[]{:S(2)}) async-start(), calls=%async_computation.6 | async-start | bytes 2228224
  87.1 1.6 copy-start.8
  87.1 1.6 copy-start.9
  93.0 3.4 copy-start
  102.8 2.8 copy-start.4
  112.7 2.4 copy-start.1
  117.9 1.3 copy-start.2
  121.2 1.6 copy-start.3
  121.2 228.9 %reduce-scatter.5.cloned.1.call-start = ((), (), s32[]{:S(2)}) async-start(), calls=%async_computation.5 | async-start | bytes 2228224 | tf_op jit(solution)/shard_map/reduce_scatter | solution.py:89
  124.3 105.6 %all-to-all-start.1 = ((f32[1,16,128]{2,0,1:T(1,128)}), f32[1,16,128]{2,0,1:T(1,128)S(1)}, u32[]{:S(2)}, u32[]{:S(2)}) async-start(f32[1,16,128]{2,0,1:T(1,128)} %bitcast.7), calls=%async_computation.2 | async-start | bytes 16384 | tf_op jit(solution)/shard_map/all_to_all | solution.py:36
Sparse Core Ops, SparseCore 0:
  24.5 59.7 all-gather.1
  121.4 168.6 reduce-scatter.6
  292.7 57.3 reduce-scatter.4
where the time goes:
time: 361 us; the launch traced here: 358 us
  waiting for transfers between devices  175 us (48%)
  starting transfers between devices  109 us (30%)
  local copies, waits for them, and re-layouts  33.3 us (9%)
  matrix products  18.7 us (5%)
  between operations  14.5 us (4%)
  other arithmetic  7.95 us (2%)
    all_to_all x1, starting transfers between devices, body(): lax.all_to_all(moving_scale, 'track', split_axis=1, concat_axis=0, tiled=...  98.6 us
    unnamed x4, waiting for transfers between devices  60.2 us
    reduce_scatter x1, waiting for transfers between devices, body(): lax.psum_scatter(user_sums, 'track', scatter_dimension=0, tiled=True)  58.4 us
    all_to_all x1, waiting for transfers between devices, body(): lax.all_to_all(moving, 'track', split_axis=1, concat_axis=0, tiled=True)  46.5 us
    unnamed x15, local copies, waits for them, and re-layouts  15.2 us
    while x12, local copies, waits for them, and re-layouts  10.9 us
    all_to_all x1, starting transfers between devices, body(): lax.all_to_all(moving, 'track', split_axis=1, concat_axis=0, tiled=True)  10.1 us
  transfers between devices with their start and end apart: 5, of which 5 were waited for; matrix products, arithmetic and copies ran while one was open for 4% of the time, Pallas kernels for 0%

commit v1 on v0

v1 whole, which is shorter than its diff:
```python
import jax
import jax.numpy as jnp
from jax import lax
from jax.experimental import pallas as pl
from jax.experimental.pallas import tpu as pltpu
from jax.sharding import PartitionSpec as P

TILE = 128
TILES = 16
EMB = 128
SLOTS = 128
SLOT_STEP = 16
BLOCK = 256
MIB = 1 << 20
F32 = jnp.float32
BF16 = jnp.bfloat16


def rows_of(i, size):
    return pl.ds(pl.multiple_of(i * size, size), size)


def split_hi_lo(x):
    hi = x.astype(BF16)
    return hi, (x - hi.astype(F32)).astype(BF16)


def build_kernel(row_ref, col_ref, count_ref, vals_ref, hi_ref, lo_ref, slots, dense, hi, lo, sems):
    loads = SLOTS // SLOT_STEP
    copies = []
    for i in range(loads):
        part = pl.ds(i * SLOT_STEP, SLOT_STEP)
        copies.append(pltpu.make_async_copy(vals_ref.at[part], slots.at[part], sems.at[i]))
        copies[-1].start()

    def clear(i, carry):
        dense[i] = jnp.zeros((TILE, TILE), F32)
        return carry

    lax.fori_loop(0, TILES * TILES, clear, 0)

    def add(s, carry):
        dense[row_ref[s] * TILES + col_ref[s]] += slots[s]
        return carry

    for i in range(loads):
        copies[i].wait()
        live = jnp.clip(count_ref[0], i * SLOT_STEP, (i + 1) * SLOT_STEP)
        lax.fori_loop(i * SLOT_STEP, live, add, 0)

    copies = []
    for b in range(SIZE // BLOCK):

        def pack(r, carry):
            rows = rows_of(r, TILE)
            for c in range(TILES):
                high, low = split_hi_lo(dense[r * TILES + c])
                hi[rows, c * TILE : (c + 1) * TILE] = high
                lo[rows, c * TILE : (c + 1) * TILE] = low
            return carry

        lax.fori_loop(2 * b, 2 * b + 2, pack, 0)
        rows = pl.ds(b * BLOCK, BLOCK)
        copies.append(pltpu.make_async_copy(hi.at[rows], hi_ref.at[rows], sems.at[2 * b]))
        copies.append(pltpu.make_async_copy(lo.at[rows], lo_ref.at[rows], sems.at[2 * b + 1]))
        copies[-2].start()
        copies[-1].start()
    for copy in copies:
        copy.wait()


VMEM = pl.BlockSpec(memory_space=pltpu.VMEM)
SMEM = pl.BlockSpec(memory_space=pltpu.SMEM)
HBM = pl.BlockSpec(memory_space=pltpu.HBM)
SIZE = TILES * TILE
BLOCKS = SIZE // BLOCK
DEPTH = 3


def build(vals, rows, cols, count):
    return pl.pallas_call(
        build_kernel,
        in_specs=[SMEM, SMEM, SMEM, HBM],
        out_specs=[HBM, HBM],
        out_shape=[jax.ShapeDtypeStruct((SIZE, SIZE), BF16)] * 2,
        scratch_shapes=[
            pltpu.VMEM((SLOTS, TILE, TILE), F32),
            pltpu.VMEM((TILES * TILES, TILE, TILE), F32),
            pltpu.VMEM((SIZE, SIZE), BF16),
            pltpu.VMEM((SIZE, SIZE), BF16),
            pltpu.SemaphoreType.DMA((2 * BLOCKS,)),
        ],
        compiler_params=pltpu.CompilerParams(vmem_limit_bytes=48 * MIB),
        cost_estimate=pl.CostEstimate(flops=0, bytes_accessed=24 * MIB, transcendentals=0),
    )(rows, cols, count, vals)


def stream(hi_ref, lo_ref, hi, lo, sems, part):
    def copies(b):
        at = part(b)
        return [
            pltpu.make_async_copy(hi_ref.at[at], hi.at[at], sems.at[0, b]),
            pltpu.make_async_copy(lo_ref.at[at], lo.at[at], sems.at[1, b]),
        ]

    def begin(b):
        for copy in copies(b):
            copy.start()

    def finish(b):
        for copy in copies(b):
            copy.wait()

        @pl.when(b + DEPTH < BLOCKS)
        def _():
            begin(b + DEPTH)

    for b in range(DEPTH):
        begin(b)
    return finish


def track_kernel(place_ref, *refs):
    blocks, (theirs_ref, hi_ref, lo_ref, out_ref, phi, plo, hi, lo, sems) = refs[:8], refs[8:]
    core = place_ref[1]
    finish = stream(
        hi_ref, lo_ref, hi, lo, sems, lambda b: (slice(None), rows_of(b, BLOCK))
    )

    def put(tile, x):
        high, low = split_hi_lo(x.T)
        at = rows_of(tile, TILE)
        phi[:, at] = high
        plo[:, at] = low

    for d in range(8):
        z = lax.rem(place_ref[0] + d, 8)
        put(2 * z + core, blocks[d][...])
        put(2 * z + 1 - core, theirs_ref[d])

    def one(b, carry):
        at = rows_of(b, BLOCK)
        finish(b)
        out = jnp.dot(phi[...], hi[:, at], preferred_element_type=F32)
        out += jnp.dot(plo[...], hi[:, at], preferred_element_type=F32)
        out += jnp.dot(phi[...], lo[:, at], preferred_element_type=F32)
        out_ref[at, :] = out.T
        return carry

    lax.fori_loop(0, BLOCKS, one, 0)


STREAM = [pltpu.VMEM((SIZE, SIZE), BF16)] * 2 + [pltpu.SemaphoreType.DMA((2, BLOCKS))]


def cost(flops):
    return pl.CostEstimate(flops=flops, bytes_accessed=1024, transcendentals=0)


def track_sums(place, blocks, theirs, hi, lo):
    return pl.pallas_call(
        track_kernel,
        in_specs=[SMEM] + [VMEM] * 9 + [HBM] * 2,
        out_specs=VMEM,
        scratch_shapes=[pltpu.VMEM((2 * EMB, SIZE), BF16)] * 2 + STREAM,
        out_shape=jax.ShapeDtypeStruct((SIZE, 2 * EMB), F32),
        compiler_params=pltpu.CompilerParams(vmem_limit_bytes=56 * MIB),
        cost_estimate=cost(0),
    )(place, *blocks, theirs, hi, lo)


def user_kernel(place_ref, *refs):
    embs, cots = refs[:4], refs[4:8]
    hi_ref, lo_ref, keep_ref, send_ref, phi, plo, sums, hi, lo, sems = refs[8:]
    share = TILE // 4

    def block(b):
        return rows_of(lax.rem(place_ref[0] + b, 8), BLOCK)

    finish = stream(hi_ref, lo_ref, hi, lo, sems, lambda b: (block(b), slice(None)))

    def put(pieces, start, lanes):
        for d in range(4):
            at = rows_of(lax.rem(start + d, 4), share)

            def tile(c, carry):
                high, low = split_hi_lo(pieces[d][c])
                phi[c, at, lanes] = high
                plo[c, at, lanes] = low
                return carry

            lax.fori_loop(0, TILES, tile, 0, unroll=4)

    put(embs, place_ref[3], slice(0, EMB))
    put(cots, place_ref[2], slice(EMB, 2 * EMB))
    core = place_ref[1]

    def one(b, carry):
        at = block(b)
        finish(b)
        panel_hi = phi[...].reshape(SIZE, 2 * EMB)
        out = jnp.dot(hi[at, :], panel_hi, preferred_element_type=F32)
        out += jnp.dot(lo[at, :], panel_hi, preferred_element_type=F32)
        panel_lo = plo[...].reshape(SIZE, 2 * EMB)
        out += jnp.dot(hi[at, :], panel_lo, preferred_element_type=F32)
        sums[...] = out
        keep_ref[b] = sums[rows_of(core, TILE), :]
        send_ref[b] = sums[rows_of(1 - core, TILE), :]
        return carry

    lax.fori_loop(0, BLOCKS, one, 0)


def user_sums(place, embs, cots, hi, lo):
    return pl.pallas_call(
        user_kernel,
        in_specs=[SMEM] + [VMEM] * 8 + [HBM] * 2,
        out_specs=[VMEM] * 2,
        scratch_shapes=[
            pltpu.VMEM((TILES, TILE, 2 * EMB), BF16),
            pltpu.VMEM((TILES, TILE, 2 * EMB), BF16),
            pltpu.VMEM((BLOCK, 2 * EMB), F32),
        ]
        + STREAM,
        out_shape=[jax.ShapeDtypeStruct((8, TILE, 2 * EMB), F32)] * 2,
        compiler_params=pltpu.CompilerParams(vmem_limit_bytes=56 * MIB),
        cost_estimate=cost(0),
    )(place, *embs, *cots, hi, lo)


def shift_z(x, by):
    pairs = [(2 * z + c, 2 * ((z + by) % 8) + c) for z in range(8) for c in range(2)]
    return lax.ppermute(x, "track", pairs)


def swap_core(x):
    return lax.ppermute(x, "track", [(t, t ^ 1) for t in range(16)])


def shift_x(x, by):
    pairs = [(4 * j + i, 4 * j + (i + by) % 4) for j in range(4) for i in range(4)]
    return lax.ppermute(x, "user", pairs)


def shift_y(x, by):
    pairs = [(4 * j + i, 4 * ((j + by) % 4) + i) for j in range(4) for i in range(4)]
    return lax.ppermute(x, "user", pairs)


def from_all(shift, x):
    far, right, left = shift(x, 2), shift(x, -1), shift(x, 1)
    return [x, right, far, left]


def body(
    user_emb,
    user_cot,
    track_emb,
    track_cot,
    user_degree,
    track_degree,
    tile_vals,
    tile_rows,
    tile_cols,
    tile_count,
):
    user = lax.axis_index("user").astype(jnp.int32)
    track = lax.axis_index("track").astype(jnp.int32)
    place = jnp.stack([track // 2, track % 2, user // 4, user % 4])
    user_scale = 1.0 / jnp.sqrt(user_degree.astype(F32))
    track_scale = 1.0 / jnp.sqrt(track_degree.astype(F32))

    share = TILE // 4
    scales = track_scale.reshape(TILES, TILE, 1)

    def part(x, which):
        x = x.reshape(TILES, TILE, EMB) * scales
        return lax.dynamic_slice_in_dim(x, which * share, share, 1)

    moving = jnp.concatenate(
        [part(track_emb, user % 4), part(track_cot, user // 4), scales.reshape(TILES, 1, TILE)],
        axis=1,
    )
    arrived = lax.all_to_all(moving, "track", split_axis=0, concat_axis=0, tiled=True)

    user_piece = jnp.concatenate([user_emb, user_cot], axis=1) * user_scale[:, None]
    hi, lo = build(
        tile_vals.reshape(SLOTS, TILE, TILE),
        tile_rows.reshape(SLOTS),
        tile_cols.reshape(SLOTS),
        tile_count.reshape(1),
    )
    blocks = [user_piece] + [None] * 7
    for d in range(1, 5):
        blocks[d] = shift_z(blocks[d - 1], -1)
        if d < 4:
            blocks[8 - d] = shift_z(blocks[(9 - d) % 8], 1)
        if d == 1:
            blocks[1], blocks[7], hi = lax.optimization_barrier((blocks[1], blocks[7], hi))
    arrived, hi = lax.optimization_barrier((arrived, hi))
    own_scale = lax.dynamic_slice_in_dim(arrived[:, 2 * share], user, 1, 0).reshape(TILE, 1)
    embs = from_all(shift_x, arrived[:, :share])
    cots = from_all(shift_y, arrived[:, share : 2 * share])

    mine, embs, cots = lax.optimization_barrier((jnp.stack(blocks), embs, cots))
    theirs = swap_core(mine)
    to_tracks = track_sums(place, blocks, theirs, hi, lo)
    to_tracks, embs, cots = lax.optimization_barrier((to_tracks, embs, cots))
    landed = lax.all_to_all(
        to_tracks.reshape(TILES, TILE, 2 * EMB), "user", split_axis=0, concat_axis=0, tiled=True
    )

    keep, send = user_sums(place, embs, cots, hi, lo)
    got = swap_core(send)
    up = shift_z(keep[4] + got[4], 1)
    down = shift_z(keep[5] + got[5], -1)
    for d in (3, 2, 1):
        up = up + (keep[d] + got[d])
        if d == 1:
            up, landed = lax.optimization_barrier((up, landed))
        up = shift_z(up, 1)
        if d > 1:
            down = shift_z(down + (keep[9 - d] + got[9 - d]), -1)
    user_total = (keep[0] + got[0] + up + down) * user_scale[:, None]
    track_total = (jnp.sum(landed, axis=0) * own_scale).reshape(1, 1, TILE, 2 * EMB)
    return (
        user_total[:, :EMB],
        user_total[:, EMB:],
        track_total[..., :EMB],
        track_total[..., EMB:],
    )


def solution(mesh):
    placed = (
        P(("user", "track"), None),
        P(("user", "track"), None),
        P("track", None),
        P("track", None),
        P(("user", "track")),
        P("track"),
        P("user", "track", None, None, None),
        P("user", "track", None),
        P("user", "track", None),
        P("user", "track"),
    )
    return jax.shard_map(
        body,
        mesh=mesh,
        in_specs=placed,
        out_specs=(
            P(("user", "track"), None),
            P(("user", "track"), None),
            P("user", "track", None, None),
            P("user", "track", None, None),
        ),
        check_vma=False,
    )
```

time: 361 us -> 146 us (0.40)
  waiting for transfers between devices: 175 us -> 35.8 us
  starting transfers between devices: 109 us -> 49.4 us
  Pallas kernels: 0 us -> 36.9 us
  local copies, waits for them, and re-layouts: 33.3 us -> 9.86 us
  matrix products: 18.7 us -> 0 us
  between operations: 14.5 us -> 1.62 us
    all_to_all x2, starting transfers between devices: 109 us -> 15.6 us  [the longest x1 9.98 us: body(): lax.all_to_all(moving, 'track', split_axis=0, concat_axis=0, tiled=True)]
    unnamed x4 -> x0, waiting for transfers between devices: 60.2 us -> none
    reduce_scatter x1 -> x0, waiting for transfers between devices: 58.4 us -> none  [body(): lax.psum_scatter(user_sums, 'track', scatter_dimension=0, tiled=True)]
    all_to_all x2, waiting for transfers between devices: 53.4 us -> 8.99 us  [the longest x1 8.99 us: body(): lax.all_to_all(to_tracks.reshape(TILES, TILE, 2 * EMB), 'user', split_axi...]
    pallas_call x0 -> x3, Pallas kernels: none -> 36.9 us  [the longest x1 13.9 us: track_sums(): pl.pallas_call(track_kernel, in_specs=[SMEM] + [VMEM] * 9 + [HBM] * 2, ou...]
    ppermute x0 -> x22, starting transfers between devices: none -> 33.8 us  [the longest x14 18.1 us: shift_z(): return lax.ppermute(x, 'track', pairs)]
    ppermute x0 -> x22, waiting for transfers between devices: none -> 26.8 us  [the longest x14 20 us: shift_z(): return lax.ppermute(x, 'track', pairs)]
    dot_general x6 -> x0, matrix products: 18.7 us -> none  [the longest x1 3.95 us: one_block(): jnp.einsum('kij,kje->kie', block_values, from_tracks, precision=highest)]
  transfers between devices with their start and end apart: 5 -> 24, of which waited for: 5 -> 11; matrix products, arithmetic and copies ran while one was open for 4% -> 9% of each run, Pallas kernels for 0% -> 7%
where the time goes in v1:
time: 146 us; the launch traced here: 145 us
  starting transfers between devices  49.4 us (34%)
  Pallas kernels  36.9 us (25%)
  waiting for transfers between devices  35.8 us (25%)
  other arithmetic  11.5 us (8%)
  local copies, waits for them, and re-layouts  9.86 us (7%)
  between operations  1.62 us (1%)
    ppermute x14, waiting for transfers between devices, shift_z(): return lax.ppermute(x, 'track', pairs)  20 us
    ppermute x14, starting transfers between devices, shift_z(): return lax.ppermute(x, 'track', pairs)  18.1 us
    pallas_call x1, Pallas kernels, track_sums(): pl.pallas_call(track_kernel, in_specs=[SMEM] + [VMEM] * 9 + [HBM] * 2, ou...  13.9 us
    pallas_call x1, Pallas kernels, user_sums(): pl.pallas_call(user_kernel, in_specs=[SMEM] + [VMEM] * 8 + [HBM] * 2, out...  12.6 us
    pallas_call x1, Pallas kernels, build(): pl.pallas_call(build_kernel, in_specs=[SMEM, SMEM, SMEM, HBM], out_specs=...  10.4 us
    all_to_all x1, starting transfers between devices, body(): lax.all_to_all(moving, 'track', split_axis=0, concat_axis=0, tiled=True)  9.98 us
    all_to_all x1, waiting for transfers between devices, body(): lax.all_to_all(to_tracks.reshape(TILES, TILE, 2 * EMB), 'user', split_axi...  8.99 us
    unnamed x48, local copies, waits for them, and re-layouts  7.76 us
  transfers between devices with their start and end apart: 24, of which 11 were waited for; matrix products, arithmetic and copies ran while one was open for 9% of the time, Pallas kernels for 7%

profile of v1, /device:TPU:1, one launch (start us, length us, event | category | flops | bytes accessed | tf_op | source)
XLA Modules:
  0.0 145.2 jit_solution(1575309039301226336)
XLA Ops:
  3.6 10.0 %all-to-all-start = ((f32[16,65,128]{2,1,0:T(8,128)}), f32[16,65,128]{2,1,0:T(8,128)S(1)}, u32[]{:S(2)}, u32[]{:S(2)}) async-start(f32[16,65,128]{2,1,0:T(8,128)} %pad_maximum_fusion), calls=%async_computation | async-start | bytes 1179648 | tf_op jit(solution)/shard_map/all_to_all | solution.py:284
  15.2 1.5 %collective-permute-start.1 = (f32[128,256]{1,0:T(8,128)S(1)}, f32[128,256]{1,0:T(8,128)S(1)}, u32[]{:S(2)}, u32[]{:S(2)}) collective-permute-start(f32[128,256]{1,0:T(8,128)S(1)} %maximum_multiply_fusion.refs_0_), channel_id=1, source_target_pairs={{0,2},{1,3},{2,4},{3,5},{4,6},{5,7},{6,8},{7,9},{8,10},{9,11},{10,... | collective-permute-start | bytes 393224 | tf_op jit(solution)/shard_map/ppermute | solution.py:233
  19.9 10.4 %shard_map.129 = (bf16[2048,2048]{1,0:T(8,128)(2,1)}, bf16[2048,2048]{1,0:T(8,128)(2,1)}) custom-call(s32[128]{0:T(128)S(1)} %bitcast.67, s32[128]{0:T(128)S(1)} %bitcast.68, s32[1]{0:T(128)} %bitcast.66.count_ref, f32[128,128,128]{2,1,0:T(8,128)} %bitcast.69), custom_call_target="tpu_custom_call" | custom-call | bytes 25165824 | tf_op jit(solution)/shard_map/pallas_call | solution.py:81
  31.1 1.5 %collective-permute-done.1.refs_7_ = f32[128,256]{1,0:T(8,128)S(1)} collective-permute-done((f32[128,256]{1,0:T(8,128)S(1)}, f32[128,256]{1,0:T(8,128)S(1)}, u32[]{:S(2)}, u32[]{:S(2)}) %collective-permute-start.1) | collective-permute-done | bytes 131104 | tf_op jit(solution)/shard_map/ppermute | solution.py:233
  34.8 2.0 %collective-permute-done.2.refs_2_ = f32[128,256]{1,0:T(8,128)S(1)} collective-permute-done((f32[128,256]{1,0:T(8,128)S(1)}, f32[128,256]{1,0:T(8,128)S(1)}, u32[]{:S(2)}, u32[]{:S(2)}) %collective-permute-start.2) | collective-permute-done | bytes 131104 | tf_op jit(solution)/shard_map/ppermute | solution.py:233
  36.8 2.4 %collective-permute-start.3 = (f32[128,256]{1,0:T(8,128)S(1)}, f32[128,256]{1,0:T(8,128)S(1)}, u32[]{:S(2)}, u32[]{:S(2)}) collective-permute-start(f32[128,256]{1,0:T(8,128)S(1)} %collective-permute-done.2.refs_2_), channel_id=1, source_target_pairs={{0,14},{1,15},{2,0},{3,1},{4,2},{5,3},{6,4},{7,5},{8,6},{9,7},{10,... | collective-permute-start | bytes 393224 | tf_op jit(solution)/shard_map/ppermute | solution.py:233
  41.1 3.1 %collective-permute-start.4 = (f32[128,256]{1,0:T(8,128)S(1)}, f32[128,256]{1,0:T(8,128)S(1)}, u32[]{:S(2)}, u32[]{:S(2)}) collective-permute-start(f32[128,256]{1,0:T(8,128)S(1)} %collective-permute-done.3.refs_3_), channel_id=1, source_target_pairs={{0,14},{1,15},{2,0},{3,1},{4,2},{5,3},{6,4},{7,5},{8,6},{9,7},{10,... | collective-permute-start | bytes 393224 | tf_op jit(solution)/shard_map/ppermute | solution.py:233
  47.8 2.7 %collective-permute-start.11 = (f32[16,32,128]{2,1,0:T(8,128)S(1)}, f32[16,32,128]{2,1,0:T(8,128)S(1)}, u32[]{:S(2)}, u32[]{:S(2)}) collective-permute-start(f32[16,32,128]{2,1,0:T(8,128)S(1)} %get-tuple-element.53.refs_4_), channel_id=1, source_target_pairs={{0,128},{16,144},{32,160},{48,176},{64,192},{80,208},{96,224},{112... | collective-permute-start | bytes 786440 | tf_op jit(solution)/shard_map/ppermute | solution.py:247
  52.7 2.5 %collective-permute-start.8 = (f32[16,32,128]{2,1,0:T(8,128)S(1)}, f32[16,32,128]{2,1,0:T(8,128)S(1)}, u32[]{:S(2)}, u32[]{:S(2)}) collective-permute-start(f32[16,32,128]{2,1,0:T(8,128)S(1)} %get-tuple-element.49.refs_0_), channel_id=1, source_target_pairs={{0,32},{16,48},{32,0},{48,16},{64,96},{80,112},{96,64},{112,80},{1... | collective-permute-start | bytes 786440 | tf_op jit(solution)/shard_map/ppermute | solution.py:242
  57.6 2.6 %collective-permute-done.10.refs_5_ = f32[16,32,128]{2,1,0:T(8,128)S(1)} collective-permute-done((f32[16,32,128]{2,1,0:T(8,128)S(1)}, f32[16,32,128]{2,1,0:T(8,128)S(1)}, u32[]{:S(2)}, u32[]{:S(2)}) %collective-permute-start.10) | collective-permute-done | bytes 262176 | tf_op jit(solution)/shard_map/ppermute | solution.py:247
  60.2 2.4 %collective-permute-done.8.refs_2_ = f32[16,32,128]{2,1,0:T(8,128)S(1)} collective-permute-done((f32[16,32,128]{2,1,0:T(8,128)S(1)}, f32[16,32,128]{2,1,0:T(8,128)S(1)}, u32[]{:S(2)}, u32[]{:S(2)}) %collective-permute-start.8) | collective-permute-done | bytes 262176 | tf_op jit(solution)/shard_map/ppermute | solution.py:242
  64.0 5.4 %collective-permute-start.13 = (f32[8,128,256]{2,1,0:T(8,128)}, f32[8,128,256]{2,1,0:T(8,128)S(1)}, u32[]{:S(2)}, u32[]{:S(2)}) collective-permute-start(f32[8,128,256]{2,1,0:T(8,128)} %bitcast_dynamic-update-slice_fusion), channel_id=1, source_target_pairs={{0,1},{1,0},{2,3},{3,2},{4,5},{5,4},{6,7},{7,6},{8,9},{9,8},{10,11... | collective-permute-start | bytes 3145736 | tf_op jit(solution)/shard_map/ppermute | solution.py:237
  70.1 1.8 %collective-permute-done.13.refs_8_ = f32[8,128,256]{2,1,0:T(8,128)S(1)} collective-permute-done((f32[8,128,256]{2,1,0:T(8,128)}, f32[8,128,256]{2,1,0:T(8,128)S(1)}, u32[]{:S(2)}, u32[]{:S(2)}) %collective-permute-start.13) | collective-permute-done | bytes 1048608 | tf_op jit(solution)/shard_map/ppermute | solution.py:237
  72.9 13.9 %shard_map.130 = f32[2048,256]{1,0:T(8,128)} custom-call(s32[4]{0:T(128)} %pad_add_fusion.place_ref, f32[128,256]{1,0:T(8,128)} %copy-done.5, f32[128,256]{1,0:T(8,128)} %copy-done.7, f32[128,256]{1,0:T(8,128)} %copy-done.8, f32[128,256]{1,0:T(8,128)} %copy-done.10, f32[128,256]{1,0:T(8,128)} %copy-done.12, f32[128,256]{1,0:T(8,128)} %copy-done.11, ...), custom_call_target="tpu_custom_call" | custom-call | bytes 1024 | tf_op jit(solution)/shard_map/pallas_call | solution.py:161
  86.8 12.6 %shard_map.131 = (f32[8,128,256]{2,1,0:T(8,128)}, f32[8,128,256]{2,1,0:T(8,128)}) custom-call(s32[4]{0:T(128)} %pad_add_fusion.place_ref, f32[16,32,128]{2,1,0:T(8,128)} %copy-done.3, f32[16,32,128]{2,1,0:T(8,128)} %copy-done.18, f32[16,32,128]{2,1,0:T(8,128)} %copy-done.17, f32[16,32,128]{2,1,0:T(8,128)} %copy-done.16, f32[16,32,128]{2,1,0:T(8,128)} %copy-done.2, ...), custom_call_target="tpu_custom_call" | custom-call | bytes 1024 | tf_op jit(solution)/shard_map/pallas_call | solution.py:215
  99.9 5.6 %all-to-all-start.1 = ((f32[16,128,256]{2,1,0:T(8,128)}), f32[16,128,256]{2,1,0:T(8,128)S(1)}, u32[]{:S(2)}, u32[]{:S(2)}) async-start(f32[16,128,256]{2,1,0:T(8,128)} %bitcast.26), calls=%async_computation.1 | async-start | bytes 4194304 | tf_op jit(solution)/shard_map/all_to_all | solution.py:309
  106.7 2.7 %collective-permute-start.19 = (f32[128,256]{1,0:T(8,128)S(1)}, f32[128,256]{1,0:T(8,128)S(1)}, u32[]{:S(2)}, u32[]{:S(2)}) collective-permute-start(f32[128,256]{1,0:T(8,128)S(1)} %get-tuple-element.67), channel_id=1, source_target_pairs={{0,14},{1,15},{2,0},{3,1},{4,2},{5,3},{6,4},{7,5},{8,6},{9,7},{10,... | collective-permute-start | bytes 393224 | tf_op jit(solution)/shard_map/ppermute | solution.py:233
  109.4 3.2 %collective-permute-done.15 = f32[128,256]{1,0:T(8,128)S(1)} collective-permute-done((f32[128,256]{1,0:T(8,128)S(1)}, f32[128,256]{1,0:T(8,128)S(1)}, u32[]{:S(2)}, u32[]{:S(2)}) %collective-permute-start.15) | collective-permute-done | bytes 131104 | tf_op jit(solution)/shard_map/ppermute | solution.py:233
  113.7 5.3 %collective-permute-done.16 = f32[128,256]{1,0:T(8,128)S(1)} collective-permute-done((f32[128,256]{1,0:T(8,128)S(1)}, f32[128,256]{1,0:T(8,128)S(1)}, u32[]{:S(2)}, u32[]{:S(2)}) %collective-permute-start.16) | collective-permute-done | bytes 131104 | tf_op jit(solution)/shard_map/ppermute | solution.py:233
  120.2 2.7 %collective-permute-start.20 = (f32[128,256]{1,0:T(8,128)S(1)}, f32[128,256]{1,0:T(8,128)S(1)}, u32[]{:S(2)}, u32[]{:S(2)}) collective-permute-start(f32[128,256]{1,0:T(8,128)S(1)} %get-tuple-element.65), channel_id=1, source_target_pairs={{0,14},{1,15},{2,0},{3,1},{4,2},{5,3},{6,4},{7,5},{8,6},{9,7},{10,... | collective-permute-start | bytes 393224 | tf_op jit(solution)/shard_map/ppermute | solution.py:233
  122.9 2.6 %collective-permute-done.17 = f32[128,256]{1,0:T(8,128)S(1)} collective-permute-done((f32[128,256]{1,0:T(8,128)S(1)}, f32[128,256]{1,0:T(8,128)S(1)}, u32[]{:S(2)}, u32[]{:S(2)}) %collective-permute-start.17) | collective-permute-done | bytes 131104 | tf_op jit(solution)/shard_map/ppermute | solution.py:233
  126.7 2.7 %collective-permute-start.21 = (f32[128,256]{1,0:T(8,128)S(1)}, f32[128,256]{1,0:T(8,128)S(1)}, u32[]{:S(2)}, u32[]{:S(2)}) collective-permute-start(f32[128,256]{1,0:T(8,128)S(1)} %get-tuple-element.63), channel_id=1, source_target_pairs={{0,14},{1,15},{2,0},{3,1},{4,2},{5,3},{6,4},{7,5},{8,6},{9,7},{10,... | collective-permute-start | bytes 393224 | tf_op jit(solution)/shard_map/ppermute | solution.py:233
  129.4 9.0 %all-to-all-done.1 = f32[16,128,256]{2,1,0:T(8,128)S(1)} async-done(((f32[16,128,256]{2,1,0:T(8,128)}), f32[16,128,256]{2,1,0:T(8,128)S(1)}, u32[]{:S(2)}, u32[]{:S(2)}) %all-to-all-start.1) | async-done | bytes 2097184 | tf_op jit(solution)/shard_map/all_to_all | solution.py:309
  139.3 4.1 %collective-permute-done.18 = f32[128,256]{1,0:T(8,128)S(1)} collective-permute-done((f32[128,256]{1,0:T(8,128)S(1)}, f32[128,256]{1,0:T(8,128)S(1)}, u32[]{:S(2)}, u32[]{:S(2)}) %collective-permute-start.18) | collective-permute-done | bytes 131104 | tf_op jit(solution)/shard_map/ppermute | solution.py:233
  (96 shorter events, 30.9 us)
Async XLA Ops:
  3.6 41.3 %all-to-all-start = ((f32[16,65,128]{2,1,0:T(8,128)}), f32[16,65,128]{2,1,0:T(8,128)S(1)}, u32[]{:S(2)}, u32[]{:S(2)}) async-start(f32[16,65,128]{2,1,0:T(8,128)} %pad_maximum_fusion), calls=%async_computation | async-start | bytes 1179648 | tf_op jit(solution)/shard_map/all_to_all | solution.py:284
  15.2 17.4 %collective-permute-start.1 = (f32[128,256]{1,0:T(8,128)S(1)}, f32[128,256]{1,0:T(8,128)S(1)}, u32[]{:S(2)}, u32[]{:S(2)}) collective-permute-start(f32[128,256]{1,0:T(8,128)S(1)} %maximum_multiply_fusion.refs_0_), channel_id=1, source_target_pairs={{0,2},{1,3},{2,4},{3,5},{4,6},{5,7},{6,8},{7,9},{8,10},{9,11},{10,... | collective-permute-start | bytes 393224 | tf_op jit(solution)/shard_map/ppermute | solution.py:233
  16.7 15.9 %collective-permute-start = (f32[128,256]{1,0:T(8,128)S(1)}, f32[128,256]{1,0:T(8,128)S(1)}, u32[]{:S(2)}, u32[]{:S(2)}) collective-permute-start(f32[128,256]{1,0:T(8,128)S(1)} %maximum_multiply_fusion.refs_0_), channel_id=1, source_target_pairs={{0,14},{1,15},{2,0},{3,1},{4,2},{5,3},{6,4},{7,5},{8,6},{9,7},{10,... | collective-permute-start | bytes 393224 | tf_op jit(solution)/shard_map/ppermute | solution.py:233
  32.6 4.2 %collective-permute-start.2 = (f32[128,256]{1,0:T(8,128)S(1)}, f32[128,256]{1,0:T(8,128)S(1)}, u32[]{:S(2)}, u32[]{:S(2)}) collective-permute-start(f32[128,256]{1,0:T(8,128)S(1)} %collective-permute-done.refs_1_), channel_id=1, source_target_pairs={{0,14},{1,15},{2,0},{3,1},{4,2},{5,3},{6,4},{7,5},{8,6},{9,7},{10,... | collective-permute-start | bytes 393224 | tf_op jit(solution)/shard_map/ppermute | solution.py:233
  33.8 5.4 %collective-permute-start.5 = (f32[128,256]{1,0:T(8,128)S(1)}, f32[128,256]{1,0:T(8,128)S(1)}, u32[]{:S(2)}, u32[]{:S(2)}) collective-permute-start(f32[128,256]{1,0:T(8,128)S(1)} %collective-permute-done.1.refs_7_), channel_id=1, source_target_pairs={{0,2},{1,3},{2,4},{3,5},{4,6},{5,7},{6,8},{7,9},{8,10},{9,11},{10,... | collective-permute-start | bytes 393224 | tf_op jit(solution)/shard_map/ppermute | solution.py:233
  36.8 4.3 %collective-permute-start.3 = (f32[128,256]{1,0:T(8,128)S(1)}, f32[128,256]{1,0:T(8,128)S(1)}, u32[]{:S(2)}, u32[]{:S(2)}) collective-permute-start(f32[128,256]{1,0:T(8,128)S(1)} %collective-permute-done.2.refs_2_), channel_id=1, source_target_pairs={{0,14},{1,15},{2,0},{3,1},{4,2},{5,3},{6,4},{7,5},{8,6},{9,7},{10,... | collective-permute-start | bytes 393224 | tf_op jit(solution)/shard_map/ppermute | solution.py:233
  39.2 7.9 %collective-permute-start.6 = (f32[128,256]{1,0:T(8,128)S(1)}, f32[128,256]{1,0:T(8,128)S(1)}, u32[]{:S(2)}, u32[]{:S(2)}) collective-permute-start(f32[128,256]{1,0:T(8,128)S(1)} %collective-permute-done.5.refs_6_), channel_id=1, source_target_pairs={{0,2},{1,3},{2,4},{3,5},{4,6},{5,7},{6,8},{7,9},{8,10},{9,11},{10,... | collective-permute-start | bytes 393224 | tf_op jit(solution)/shard_map/ppermute | solution.py:233
  41.1 5.2 %collective-permute-start.4 = (f32[128,256]{1,0:T(8,128)S(1)}, f32[128,256]{1,0:T(8,128)S(1)}, u32[]{:S(2)}, u32[]{:S(2)}) collective-permute-start(f32[128,256]{1,0:T(8,128)S(1)} %collective-permute-done.3.refs_3_), channel_id=1, source_target_pairs={{0,14},{1,15},{2,0},{3,1},{4,2},{5,3},{6,4},{7,5},{8,6},{9,7},{10,... | collective-permute-start | bytes 393224 | tf_op jit(solution)/shard_map/ppermute | solution.py:233
  45.0 10.1 %collective-permute-start.12 = (f32[16,32,128]{2,1,0:T(8,128)S(1)}, f32[16,32,128]{2,1,0:T(8,128)S(1)}, u32[]{:S(2)}, u32[]{:S(2)}) collective-permute-start(f32[16,32,128]{2,1,0:T(8,128)S(1)} %get-tuple-element.53.refs_4_), channel_id=1, source_target_pairs={{0,64},{16,80},{32,96},{48,112},{64,128},{80,144},{96,160},{112,17... | collective-permute-start | bytes 786440 | tf_op jit(solution)/shard_map/ppermute | solution.py:247
  47.8 9.8 %collective-permute-start.11 = (f32[16,32,128]{2,1,0:T(8,128)S(1)}, f32[16,32,128]{2,1,0:T(8,128)S(1)}, u32[]{:S(2)}, u32[]{:S(2)}) collective-permute-start(f32[16,32,128]{2,1,0:T(8,128)S(1)} %get-tuple-element.53.refs_4_), channel_id=1, source_target_pairs={{0,128},{16,144},{32,160},{48,176},{64,192},{80,208},{96,224},{112... | collective-permute-start | bytes 786440 | tf_op jit(solution)/shard_map/ppermute | solution.py:247
  50.5 9.7 %collective-permute-start.10 = (f32[16,32,128]{2,1,0:T(8,128)S(1)}, f32[16,32,128]{2,1,0:T(8,128)S(1)}, u32[]{:S(2)}, u32[]{:S(2)}) collective-permute-start(f32[16,32,128]{2,1,0:T(8,128)S(1)} %get-tuple-element.53.refs_4_), channel_id=1, source_target_pairs={{0,192},{16,208},{32,224},{48,240},{64,0},{80,16},{96,32},{112,48}... | collective-permute-start | bytes 786440 | tf_op jit(solution)/shard_map/ppermute | solution.py:247
  51.5 8.8 %collective-permute-start.9 = (f32[16,32,128]{2,1,0:T(8,128)S(1)}, f32[16,32,128]{2,1,0:T(8,128)S(1)}, u32[]{:S(2)}, u32[]{:S(2)}) collective-permute-start(f32[16,32,128]{2,1,0:T(8,128)S(1)} %get-tuple-element.49.refs_0_), channel_id=1, source_target_pairs={{0,16},{16,32},{32,48},{48,0},{64,80},{80,96},{96,112},{112,64},{1... | collective-permute-start | bytes 786440 | tf_op jit(solution)/shard_map/ppermute | solution.py:242
  52.7 9.9 %collective-permute-start.8 = (f32[16,32,128]{2,1,0:T(8,128)S(1)}, f32[16,32,128]{2,1,0:T(8,128)S(1)}, u32[]{:S(2)}, u32[]{:S(2)}) collective-permute-start(f32[16,32,128]{2,1,0:T(8,128)S(1)} %get-tuple-element.49.refs_0_), channel_id=1, source_target_pairs={{0,32},{16,48},{32,0},{48,16},{64,96},{80,112},{96,64},{112,80},{1... | collective-permute-start | bytes 786440 | tf_op jit(solution)/shard_map/ppermute | solution.py:242
  55.1 8.2 %collective-permute-start.7 = (f32[16,32,128]{2,1,0:T(8,128)S(1)}, f32[16,32,128]{2,1,0:T(8,128)S(1)}, u32[]{:S(2)}, u32[]{:S(2)}) collective-permute-start(f32[16,32,128]{2,1,0:T(8,128)S(1)} %get-tuple-element.49.refs_0_), channel_id=1, source_target_pairs={{0,48},{16,0},{32,16},{48,32},{64,112},{80,64},{96,80},{112,96},{1... | collective-permute-start | bytes 786440 | tf_op jit(solution)/shard_map/ppermute | solution.py:242
  64.0 7.9 %collective-permute-start.13 = (f32[8,128,256]{2,1,0:T(8,128)}, f32[8,128,256]{2,1,0:T(8,128)S(1)}, u32[]{:S(2)}, u32[]{:S(2)}) collective-permute-start(f32[8,128,256]{2,1,0:T(8,128)} %bitcast_dynamic-update-slice_fusion), channel_id=1, source_target_pairs={{0,1},{1,0},{2,3},{3,2},{4,5},{5,4},{6,7},{7,6},{8,9},{9,8},{10,11... | collective-permute-start | bytes 3145736 | tf_op jit(solution)/shard_map/ppermute | solution.py:237
  99.4 6.1 %collective-permute-start.14 = (f32[8,128,256]{2,1,0:T(8,128)}, f32[8,128,256]{2,1,0:T(8,128)}, u32[]{:S(2)}, u32[]{:S(2)}) collective-permute-start(f32[8,128,256]{2,1,0:T(8,128)} %get-tuple-element.58), channel_id=1, source_target_pairs={{0,1},{1,0},{2,3},{3,2},{4,5},{5,4},{6,7},{7,6},{8,9},{9,8},{10,11... | collective-permute-start | bytes 3145736 | tf_op jit(solution)/shard_map/ppermute | solution.py:237
  99.9 38.5 %all-to-all-start.1 = ((f32[16,128,256]{2,1,0:T(8,128)}), f32[16,128,256]{2,1,0:T(8,128)S(1)}, u32[]{:S(2)}, u32[]{:S(2)}) async-start(f32[16,128,256]{2,1,0:T(8,128)} %bitcast.26), calls=%async_computation.1 | async-start | bytes 4194304 | tf_op jit(solution)/shard_map/all_to_all | solution.py:309
  106.6 5.9 %collective-permute-start.15 = (f32[128,256]{1,0:T(8,128)S(1)}, f32[128,256]{1,0:T(8,128)S(1)}, u32[]{:S(2)}, u32[]{:S(2)}) collective-permute-start(f32[128,256]{1,0:T(8,128)S(1)} %get-tuple-element.66), channel_id=1, source_target_pairs={{0,2},{1,3},{2,4},{3,5},{4,6},{5,7},{6,8},{7,9},{8,10},{9,11},{10,... | collective-permute-start | bytes 393224 | tf_op jit(solution)/shard_map/ppermute | solution.py:233
  106.7 6.9 %collective-permute-start.19 = (f32[128,256]{1,0:T(8,128)S(1)}, f32[128,256]{1,0:T(8,128)S(1)}, u32[]{:S(2)}, u32[]{:S(2)}) collective-permute-start(f32[128,256]{1,0:T(8,128)S(1)} %get-tuple-element.67), channel_id=1, source_target_pairs={{0,14},{1,15},{2,0},{3,1},{4,2},{5,3},{6,4},{7,5},{8,6},{9,7},{10,... | collective-permute-start | bytes 393224 | tf_op jit(solution)/shard_map/ppermute | solution.py:233
  113.6 5.4 %collective-permute-start.16 = (f32[128,256]{1,0:T(8,128)S(1)}, f32[128,256]{1,0:T(8,128)S(1)}, u32[]{:S(2)}, u32[]{:S(2)}) collective-permute-start(f32[128,256]{1,0:T(8,128)S(1)} %fusion.10), channel_id=1, source_target_pairs={{0,2},{1,3},{2,4},{3,5},{4,6},{5,7},{6,8},{7,9},{8,10},{9,11},{10,... | collective-permute-start | bytes 393224 | tf_op jit(solution)/shard_map/ppermute | solution.py:233
  120.1 5.4 %collective-permute-start.17 = (f32[128,256]{1,0:T(8,128)S(1)}, f32[128,256]{1,0:T(8,128)S(1)}, u32[]{:S(2)}, u32[]{:S(2)}) collective-permute-start(f32[128,256]{1,0:T(8,128)S(1)} %get-tuple-element.64), channel_id=1, source_target_pairs={{0,2},{1,3},{2,4},{3,5},{4,6},{5,7},{6,8},{7,9},{8,10},{9,11},{10,... | collective-permute-start | bytes 393224 | tf_op jit(solution)/shard_map/ppermute | solution.py:233
  120.2 5.3 %collective-permute-start.20 = (f32[128,256]{1,0:T(8,128)S(1)}, f32[128,256]{1,0:T(8,128)S(1)}, u32[]{:S(2)}, u32[]{:S(2)}) collective-permute-start(f32[128,256]{1,0:T(8,128)S(1)} %get-tuple-element.65), channel_id=1, source_target_pairs={{0,14},{1,15},{2,0},{3,1},{4,2},{5,3},{6,4},{7,5},{8,6},{9,7},{10,... | collective-permute-start | bytes 393224 | tf_op jit(solution)/shard_map/ppermute | solution.py:233
  126.7 12.6 %collective-permute-start.21 = (f32[128,256]{1,0:T(8,128)S(1)}, f32[128,256]{1,0:T(8,128)S(1)}, u32[]{:S(2)}, u32[]{:S(2)}) collective-permute-start(f32[128,256]{1,0:T(8,128)S(1)} %get-tuple-element.63), channel_id=1, source_target_pairs={{0,14},{1,15},{2,0},{3,1},{4,2},{5,3},{6,4},{7,5},{8,6},{9,7},{10,... | collective-permute-start | bytes 393224 | tf_op jit(solution)/shard_map/ppermute | solution.py:233
  138.4 5.0 %collective-permute-start.18 = (f32[128,256]{1,0:T(8,128)S(1)}, f32[128,256]{1,0:T(8,128)S(1)}, u32[]{:S(2)}, u32[]{:S(2)}) collective-permute-start(f32[128,256]{1,0:T(8,128)S(1)} %get-tuple-element.60), channel_id=1, source_target_pairs={{0,2},{1,3},{2,4},{3,5},{4,6},{5,7},{6,8},{7,9},{8,10},{9,11},{10,... | collective-permute-start | bytes 393224 | tf_op jit(solution)/shard_map/ppermute | solution.py:233
  (21 other events, 472.6 us)

commit v2 on v1

v2 whole, which is shorter than its diff:
```python
import functools

import jax
import jax.numpy as jnp
from jax import lax
from jax.experimental import pallas as pl
from jax.experimental.pallas import tpu as pltpu
from jax.sharding import PartitionSpec as P

TILE = 128
TILES = 16
EMB = 128
SLOTS = 128
SLOT_STEP = 16
HALF = TILES // 2
BLOCK = 256
MIB = 1 << 20
F32 = jnp.float32
BF16 = jnp.bfloat16


def rows_of(i, size):
    return pl.ds(pl.multiple_of(i * size, size), size)


def split_hi_lo(x):
    hi = x.astype(BF16)
    return hi, (x - hi.astype(F32)).astype(BF16)


def build_kernel(half, row_ref, col_ref, count_ref, vals_ref, *refs):
    out_ref, slots, dense, hi, lo, sems = refs[-6:]
    loads = SLOTS // SLOT_STEP
    copies = []
    for i in range(loads):
        part = pl.ds(i * SLOT_STEP, SLOT_STEP)
        copies.append(pltpu.make_async_copy(vals_ref.at[part], slots.at[part], sems.at[i]))
        copies[-1].start()

    def clear(i, carry):
        dense[i] = jnp.zeros((TILE, TILE), F32)
        return carry

    lax.fori_loop(0, HALF * TILES, clear, 0)

    def add(s, carry):
        row = row_ref[s] - half * HALF

        @pl.when((row >= 0) & (row < HALF))
        def _():
            dense[row * TILES + col_ref[s]] += slots[s]

        return carry

    for i in range(loads):
        copies[i].wait()
        live = jnp.clip(count_ref[0], i * SLOT_STEP, (i + 1) * SLOT_STEP)
        lax.fori_loop(i * SLOT_STEP, live, add, 0)

    copies = []
    for b in range(HALF // 2):

        def pack(r, carry):
            rows = rows_of(r, TILE)
            for c in range(TILES):
                high, low = split_hi_lo(dense[r * TILES + c])
                hi[rows, c * TILE : (c + 1) * TILE] = high
                lo[rows, c * TILE : (c + 1) * TILE] = low
            return carry

        lax.fori_loop(2 * b, 2 * b + 2, pack, 0)
        rows = pl.ds(b * BLOCK, BLOCK)
        there = pl.ds(half * HALF * TILE + b * BLOCK, BLOCK)
        copies.append(pltpu.make_async_copy(hi.at[rows], out_ref.at[0, there], sems.at[2 * b]))
        copies.append(pltpu.make_async_copy(lo.at[rows], out_ref.at[1, there], sems.at[2 * b + 1]))
        copies[-2].start()
        copies[-1].start()
    for copy in copies:
        copy.wait()


VMEM = pl.BlockSpec(memory_space=pltpu.VMEM)
SMEM = pl.BlockSpec(memory_space=pltpu.SMEM)
HBM = pl.BlockSpec(memory_space=pltpu.HBM)
SIZE = TILES * TILE
BLOCKS = SIZE // BLOCK
DEPTH = 3
STREAM = [pltpu.SemaphoreType.DMA((DEPTH, 2))]


def cost(nbytes):
    return pl.CostEstimate(flops=0, bytes_accessed=nbytes, transcendentals=0)


def build(half, vals, rows, cols, count, *others):
    return pl.pallas_call(
        functools.partial(build_kernel, half),
        in_specs=[SMEM, SMEM, SMEM, HBM] + [HBM] * len(others),
        out_specs=HBM,
        out_shape=jax.ShapeDtypeStruct((2, SIZE, SIZE), BF16),
        input_output_aliases={4: 0} if others else {},
        scratch_shapes=[
            pltpu.VMEM((SLOTS, TILE, TILE), F32),
            pltpu.VMEM((HALF * TILES, TILE, TILE), F32),
            pltpu.VMEM((HALF * TILE, SIZE), BF16),
            pltpu.VMEM((HALF * TILE, SIZE), BF16),
            pltpu.SemaphoreType.DMA((SLOTS // SLOT_STEP,)),
        ],
        compiler_params=pltpu.CompilerParams(vmem_limit_bytes=46 * MIB),
        cost_estimate=cost(12 * MIB * half),
    )(rows, cols, count, vals, *others)


def stream(adj_ref, slots, sems, part):
    def copies(b):
        at = part(b)
        slot = lax.rem(b, DEPTH)
        return [
            pltpu.make_async_copy(adj_ref.at[(k,) + at], slots.at[slot, k], sems.at[slot, k])
            for k in range(2)
        ]

    def begin(b):
        for copy in copies(b):
            copy.start()

    def finish(b):
        for copy in copies(b):
            copy.wait()
        slot = lax.rem(b, DEPTH)
        return slots[slot, 0], slots[slot, 1]

    def after(b):
        @pl.when(b + DEPTH < BLOCKS)
        def _():
            begin(b + DEPTH)

    for b in range(DEPTH):
        begin(b)
    return finish, after


def track_kernel(*refs):
    blocks, (theirs_ref, adj_ref, out_ref, phi, plo, slots, sems) = refs[:8], refs[8:]
    track = lax.axis_index("track")
    core = lax.rem(track, 2)
    finish, after = stream(adj_ref, slots, sems, lambda b: (slice(None), rows_of(b, BLOCK)))

    def put(tile, x):
        high, low = split_hi_lo(x.T)
        at = rows_of(tile, TILE)
        phi[:, at] = high
        plo[:, at] = low

    for d in range(8):
        z = lax.rem(lax.div(track, 2) + d, 8)
        put(2 * z + core, blocks[d][...])
        put(2 * z + 1 - core, theirs_ref[d])

    def one(b, carry):
        at = rows_of(b, BLOCK)
        hi, lo = finish(b)
        out = jnp.dot(phi[...], hi, preferred_element_type=F32)
        out += jnp.dot(plo[...], hi, preferred_element_type=F32)
        out += jnp.dot(phi[...], lo, preferred_element_type=F32)
        out_ref[at, :] = out.T
        after(b)
        return carry

    lax.fori_loop(0, BLOCKS, one, 0)


def track_sums(blocks, theirs, adj):
    return pl.pallas_call(
        track_kernel,
        in_specs=[VMEM] * 9 + [HBM],
        out_specs=VMEM,
        scratch_shapes=[pltpu.VMEM((2 * EMB, SIZE), BF16)] * 2
        + [pltpu.VMEM((DEPTH, 2, SIZE, BLOCK), BF16)]
        + STREAM,
        out_shape=jax.ShapeDtypeStruct((SIZE, 2 * EMB), F32),
        compiler_params=pltpu.CompilerParams(vmem_limit_bytes=46 * MIB),
        cost_estimate=cost(MIB),
    )(*blocks, theirs, adj)


def user_kernel(panel_ref, adj_ref, keep_ref, send_ref, phi, plo, sums, slots, sems):
    track = lax.axis_index("track")
    core = lax.rem(track, 2)

    def block(b):
        return rows_of(lax.rem(lax.div(track, 2) + b, 8), BLOCK)

    finish, after = stream(adj_ref, slots, sems, lambda b: (block(b), slice(None)))

    def tile(c, carry):
        for u in range(0, TILES, 2):
            pair = jnp.concatenate([panel_ref[u, c], panel_ref[u + 1, c]], axis=0)
            high, low = split_hi_lo(pair)
            at = rows_of(c * (TILES // 2) + u // 2, 16)
            phi[at, :] = high
            plo[at, :] = low
        return carry

    lax.fori_loop(0, TILES, tile, 0)

    def one(b, carry):
        hi, lo = finish(b)
        out = jnp.dot(hi, phi[...], preferred_element_type=F32)
        out += jnp.dot(lo, phi[...], preferred_element_type=F32)
        out += jnp.dot(hi, plo[...], preferred_element_type=F32)
        sums[...] = out
        after(b)
        keep_ref[b] = sums[rows_of(core, TILE), :]
        send_ref[b] = sums[rows_of(1 - core, TILE), :]
        return carry

    lax.fori_loop(0, BLOCKS, one, 0)


def user_sums(panel, adj):
    return pl.pallas_call(
        user_kernel,
        in_specs=[VMEM, HBM],
        out_specs=[VMEM] * 2,
        scratch_shapes=[
            pltpu.VMEM((SIZE, 2 * EMB), BF16),
            pltpu.VMEM((SIZE, 2 * EMB), BF16),
            pltpu.VMEM((BLOCK, 2 * EMB), F32),
            pltpu.VMEM((DEPTH, 2, BLOCK, SIZE), BF16),
        ]
        + STREAM,
        out_shape=[jax.ShapeDtypeStruct((8, TILE, 2 * EMB), F32)] * 2,
        compiler_params=pltpu.CompilerParams(vmem_limit_bytes=46 * MIB),
        cost_estimate=cost(MIB),
    )(panel, adj)


def pack_kernel(*refs):
    for d in range(8):
        refs[8][d] = refs[d][...]


def pack(blocks):
    return pl.pallas_call(
        pack_kernel,
        in_specs=[VMEM] * 8,
        out_specs=VMEM,
        out_shape=jax.ShapeDtypeStruct((8, TILE, 2 * EMB), F32),
        compiler_params=pltpu.CompilerParams(vmem_limit_bytes=4 * MIB),
        cost_estimate=cost(2 * MIB),
    )(*blocks)


def shift_z(x, by):
    pairs = [(2 * z + c, 2 * ((z + by) % 8) + c) for z in range(8) for c in range(2)]
    return lax.ppermute(x, "track", pairs)


def swap_core(x):
    return lax.ppermute(x, "track", [(t, t ^ 1) for t in range(16)])


def body(
    user_emb,
    user_cot,
    track_emb,
    track_cot,
    user_degree,
    track_degree,
    tile_vals,
    tile_rows,
    tile_cols,
    tile_count,
):
    user = lax.axis_index("user").astype(jnp.int32)
    user_scale = 1.0 / jnp.sqrt(user_degree.astype(F32))
    track_scale = 1.0 / jnp.sqrt(track_degree.astype(F32))

    rows = TILE // TILES
    scales = track_scale.reshape(TILES, TILE, 1)

    def part(x):
        x = x.reshape(TILES, TILE, EMB) * scales
        return lax.dynamic_slice_in_dim(x, user * rows, rows, 1)

    moving = jnp.concatenate(
        [part(track_emb), part(track_cot), scales.reshape(TILES, 1, TILE)], axis=1
    )
    moving, user_emb, user_cot = lax.optimization_barrier((moving, user_emb, user_cot))
    user_piece = jnp.concatenate([user_emb, user_cot], axis=1) * user_scale[:, None]
    arrived = lax.all_to_all(moving, "track", split_axis=0, concat_axis=0, tiled=True)
    blocks = [user_piece] + [None] * 7
    for d in range(1, 4):
        blocks[d] = shift_z(blocks[d - 1], -1)
        blocks[8 - d] = shift_z(blocks[(9 - d) % 8], 1)
        if d == 2:
            tiles = (
                tile_vals.reshape(SLOTS, TILE, TILE),
                tile_rows.reshape(SLOTS),
                tile_cols.reshape(SLOTS),
                tile_count.reshape(1),
            )
            adj = build(0, *tiles)
            arrived, blocks[2], blocks[6], adj = lax.optimization_barrier(
                (arrived, blocks[2], blocks[6], adj)
            )
    blocks[4] = shift_z(blocks[3], -1)
    adj = build(1, *tiles, adj)

    scale_rows = arrived[:, 2 * rows]
    share = jnp.concatenate([arrived[:, :rows], arrived[:, rows : 2 * rows]], axis=2)
    panel = lax.all_to_all(
        jnp.broadcast_to(share, (TILES,) + share.shape), "user", split_axis=0, concat_axis=0
    )
    theirs = swap_core(pack(blocks))
    to_tracks = track_sums(blocks, theirs, adj)
    to_tracks, panel = lax.optimization_barrier((to_tracks, panel))
    keep, send = user_sums(panel, adj)
    own_scale = lax.dynamic_slice_in_dim(scale_rows, user, 1, 0).reshape(TILE, 1)
    landed = lax.all_to_all(
        to_tracks.reshape(TILES, TILE, 2 * EMB), "user", split_axis=0, concat_axis=0, tiled=True
    )
    got = swap_core(send)
    up, down = lax.optimization_barrier((keep[4] + got[4], keep[5] + got[5]))
    for d in (3, 2, 1):
        up, down = shift_z(up, 1), shift_z(down, -1)
        if d == 2:
            up, down, landed = lax.optimization_barrier((up, down, landed))
        up = up + (keep[d] + got[d])
        if d > 1:
            down = down + (keep[9 - d] + got[9 - d])
        up, down = lax.optimization_barrier((up, down))
    up = shift_z(up, 1)
    user_total = (keep[0] + got[0] + up + down) * user_scale[:, None]
    track_total = (jnp.sum(landed, axis=0) * own_scale).reshape(1, 1, TILE, 2 * EMB)
    return (
        user_total[:, :EMB],
        user_total[:, EMB:],
        track_total[..., :EMB],
        track_total[..., EMB:],
    )


def solution(mesh):
    placed = (
        P(("user", "track"), None),
        P(("user", "track"), None),
        P("track", None),
        P("track", None),
        P(("user", "track")),
        P("track"),
        P("user", "track", None, None, None),
        P("user", "track", None),
        P("user", "track", None),
        P("user", "track"),
    )
    return jax.shard_map(
        body,
        mesh=mesh,
        in_specs=placed,
        out_specs=(
            P(("user", "track"), None),
            P(("user", "track"), None),
            P("user", "track", None, None),
            P("user", "track", None, None),
        ),
        check_vma=False,
    )
```

time: 146 us -> 124 us (0.85)
  waiting for transfers between devices: 35.8 us -> 25.4 us
  local copies, waits for them, and re-layouts: 9.86 us -> 4.29 us
  other arithmetic: 11.5 us -> 6.03 us
    ppermute x6 -> x0, starting transfers between devices: 9.88 us -> none  [the longest x3 5.06 us: shift_y(): return lax.ppermute(x, 'user', pairs)]
    ppermute x14, starting transfers between devices: 18.1 us -> 25 us  [shift_z(): return lax.ppermute(x, 'track', pairs)]
    all_to_all x0 -> x1, starting transfers between devices: none -> 6.75 us  [body(): lax.all_to_all(jnp.broadcast_to(share, (TILES,) + share.shape), 'user', s...]
    unnamed x48 -> x8, local copies, waits for them, and re-layouts: 7.76 us -> 1.32 us
    ppermute x6 -> x0, waiting for transfers between devices: 5.01 us -> none  [the longest x3 2.64 us: shift_y(): return lax.ppermute(x, 'user', pairs)]
    ppermute x14, waiting for transfers between devices: 20 us -> 15.7 us  [shift_z(): return lax.ppermute(x, 'track', pairs)]
    add x3 -> x1, other arithmetic: 3.29 us -> 0.02 us  [body(): up = up + (keep[d] + got[d])]
    all_to_all x1, starting transfers between devices: 9.98 us -> 6.72 us  [body(): lax.all_to_all(moving, 'track', split_axis=0, concat_axis=0, tiled=True)]
  transfers between devices with their start and end apart: 24 -> 19, of which waited for: 11 -> 9; matrix products, arithmetic and copies ran while one was open for 9% -> 2% of each run, Pallas kernels for 7% -> 30%
where the time goes in v2:
time: 124 us
  starting transfers between devices  49 us (40%)
  Pallas kernels  37.4 us (30%)
  waiting for transfers between devices  25.4 us (20%)
  other arithmetic  6.03 us (5%)
  local copies, waits for them, and re-layouts  4.29 us (3%)
  between operations  1.5 us (1%)
    ppermute x14, starting transfers between devices, shift_z(): return lax.ppermute(x, 'track', pairs)  25 us
    ppermute x14, waiting for transfers between devices, shift_z(): return lax.ppermute(x, 'track', pairs)  15.7 us
    pallas_call x2, Pallas kernels, build(): pl.pallas_call(functools.partial(build_kernel, half), in_specs=[SMEM, SME...  15.6 us
    pallas_call x1, Pallas kernels, track_sums(): pl.pallas_call(track_kernel, in_specs=[VMEM] * 9 + [HBM], out_specs=VMEM,...  12 us
    pallas_call x1, Pallas kernels, user_sums(): pl.pallas_call(user_kernel, in_specs=[VMEM, HBM], out_specs=[VMEM] * 2, s...  9.79 us
    all_to_all x1, waiting for transfers between devices, body(): lax.all_to_all(to_tracks.reshape(TILES, TILE, 2 * EMB), 'user', split_axi...  7.31 us
    all_to_all x1, starting transfers between devices, body(): lax.all_to_all(to_tracks.reshape(TILES, TILE, 2 * EMB), 'user', split_axi...  7 us
    all_to_all x1, starting transfers between devices, body(): lax.all_to_all(jnp.broadcast_to(share, (TILES,) + share.shape), 'user', s...  6.75 us
  transfers between devices with their start and end apart: 19, of which 9 were waited for; matrix products, arithmetic and copies ran while one was open for 2% of the time, Pallas kernels for 30%

profile of v2, /device:TPU:1, one launch (start us, length us, event | category | flops | bytes accessed | tf_op | source)
XLA Modules:
  0.0 123.6 jit_solution(9106630343532008324)
XLA Ops:
  4.7 2.5 %collective-permute-start.2 = (f32[128,256]{1,0:T(8,128)S(1)}, f32[128,256]{1,0:T(8,128)S(1)}, u32[]{:S(2)}, u32[]{:S(2)}) collective-permute-start(f32[128,256]{1,0:T(8,128)S(1)} %maximum_multiply_fusion.refs_0_), channel_id=1, source_target_pairs={{0,2},{1,3},{2,4},{3,5},{4,6},{5,7},{6,8},{7,9},{8,10},{9,11},{10,... | collective-permute-start | bytes 393224 | tf_op jit(solution)/shard_map/ppermute | solution.py:257
  7.2 4.0 %collective-permute-start = (f32[128,256]{1,0:T(8,128)S(1)}, f32[128,256]{1,0:T(8,128)S(1)}, u32[]{:S(2)}, u32[]{:S(2)}) collective-permute-start(f32[128,256]{1,0:T(8,128)S(1)} %maximum_multiply_fusion.refs_0_), channel_id=1, source_target_pairs={{0,14},{1,15},{2,0},{3,1},{4,2},{5,3},{6,4},{7,5},{8,6},{9,7},{10,... | collective-permute-start | bytes 393224 | tf_op jit(solution)/shard_map/ppermute | solution.py:257
  11.3 6.7 %all-to-all-start = ((f32[16,17,128]{2,1,0:T(8,128)}), f32[16,17,128]{2,1,0:T(8,128)S(1)}, u32[]{:S(2)}, u32[]{:S(2)}) async-start(f32[16,17,128]{2,1,0:T(8,128)} %pad_maximum_fusion), calls=%async_computation | async-start | bytes 393216 | tf_op jit(solution)/shard_map/all_to_all | solution.py:292
  18.0 1.5 %collective-permute-start.3 = (f32[128,256]{1,0:T(8,128)S(1)}, f32[128,256]{1,0:T(8,128)S(1)}, u32[]{:S(2)}, u32[]{:S(2)}) collective-permute-start(f32[128,256]{1,0:T(8,128)S(1)} %collective-permute-done.2.refs_7_), channel_id=1, source_target_pairs={{0,2},{1,3},{2,4},{3,5},{4,6},{5,7},{6,8},{7,9},{8,10},{9,11},{10,... | collective-permute-start | bytes 393224 | tf_op jit(solution)/shard_map/ppermute | solution.py:257
  22.7 7.8 %shard_map.129.refs_0_ = bf16[2,2048,2048]{2,1,0:T(8,128)(2,1)} custom-call(s32[128]{0:T(128)S(1)} %bitcast.48, s32[128]{0:T(128)S(1)} %bitcast.50, s32[1]{0:T(128)} %bitcast.46.count_ref, f32[128,128,128]{2,1,0:T(8,128)} %bitcast.52), custom_call_target="tpu_custom_call" | custom-call | tf_op jit(solution)/shard_map/pallas_call | solution.py:96
  30.6 1.6 %broadcast_in_dim.2 = f32[16,16,8,256]{3,2,1,0:T(8,128)} broadcast(f32[16,8,256]{2,1,0:T(8,128)S(1)} %pad_maximum_fusion.1), dimensions={1,2,3} | broadcast | bytes 2228224 | tf_op jit(solution)/shard_map/broadcast_in_dim | solution.py:314
  32.2 6.8 %all-to-all-start.1 = ((f32[16,16,8,256]{3,2,1,0:T(8,128)}), f32[16,16,8,256]{3,2,1,0:T(8,128)S(1)}, u32[]{:S(2)}, u32[]{:S(2)}) async-start(f32[16,16,8,256]{3,2,1,0:T(8,128)} %broadcast_in_dim.2), calls=%async_computation.1 | async-start | bytes 4194304 | tf_op jit(solution)/shard_map/all_to_all | solution.py:313
  39.0 1.6 %collective-permute-start.4 = (f32[128,256]{1,0:T(8,128)S(1)}, f32[128,256]{1,0:T(8,128)S(1)}, u32[]{:S(2)}, u32[]{:S(2)}) collective-permute-start(f32[128,256]{1,0:T(8,128)S(1)} %collective-permute-done.1.refs_2_), channel_id=1, source_target_pairs={{0,14},{1,15},{2,0},{3,1},{4,2},{5,3},{6,4},{7,5},{8,6},{9,7},{10,... | collective-permute-start | bytes 393224 | tf_op jit(solution)/shard_map/ppermute | solution.py:257
  40.5 2.3 %collective-permute-done.4.refs_3_ = f32[128,256]{1,0:T(8,128)S(1)} collective-permute-done((f32[128,256]{1,0:T(8,128)S(1)}, f32[128,256]{1,0:T(8,128)S(1)}, u32[]{:S(2)}, u32[]{:S(2)}) %collective-permute-start.4) | collective-permute-done | bytes 131104 | tf_op jit(solution)/shard_map/ppermute | solution.py:257
  42.9 2.7 %collective-permute-start.5 = (f32[128,256]{1,0:T(8,128)S(1)}, f32[128,256]{1,0:T(8,128)S(1)}, u32[]{:S(2)}, u32[]{:S(2)}) collective-permute-start(f32[128,256]{1,0:T(8,128)S(1)} %collective-permute-done.4.refs_3_), channel_id=1, source_target_pairs={{0,14},{1,15},{2,0},{3,1},{4,2},{5,3},{6,4},{7,5},{8,6},{9,7},{10,... | collective-permute-start | bytes 393224 | tf_op jit(solution)/shard_map/ppermute | solution.py:257
  45.8 1.7 %collective-permute-done.5.refs_4_ = f32[128,256]{1,0:T(8,128)S(1)} collective-permute-done((f32[128,256]{1,0:T(8,128)S(1)}, f32[128,256]{1,0:T(8,128)S(1)}, u32[]{:S(2)}, u32[]{:S(2)}) %collective-permute-start.5) | collective-permute-done | bytes 131104 | tf_op jit(solution)/shard_map/ppermute | solution.py:257
  47.6 3.2 %collective-permute-start.7 = (f32[8,128,256]{2,1,0:T(8,128)S(1)}, f32[8,128,256]{2,1,0:T(8,128)S(1)}, u32[]{:S(2)}, u32[]{:S(2)}) collective-permute-start(f32[8,128,256]{2,1,0:T(8,128)S(1)} %shard_map.130), channel_id=1, source_target_pairs={{0,1},{1,0},{2,3},{3,2},{4,5},{5,4},{6,7},{7,6},{8,9},{9,8},{10,11... | collective-permute-start | bytes 3145736 | tf_op jit(solution)/shard_map/ppermute | solution.py:261
  50.7 7.8 %shard_map.131.refs_9_.adj_ref = bf16[2,2048,2048]{2,1,0:T(8,128)(2,1)} custom-call(s32[128]{0:T(128)S(1)} %bitcast.49, s32[128]{0:T(128)S(1)} %bitcast.51, s32[1]{0:T(128)} %bitcast.47.count_ref, f32[128,128,128]{2,1,0:T(8,128)} %bitcast.53, bf16[2,2048,2048]{2,1,0:T(8,128)(2,1)} %shard_map.129.refs_0_), custom_call_target="tpu_custom_call", output_to_operand_aliasing={{}: (4, {})} | custom-call | bytes 12582912 | tf_op jit(solution)/shard_map/pallas_call | solution.py:96
  58.6 12.0 %shard_map.132 = f32[2048,256]{1,0:T(8,128)} custom-call(f32[128,256]{1,0:T(8,128)S(1)} %maximum_multiply_fusion.refs_0_, f32[128,256]{1,0:T(8,128)S(1)} %collective-permute-done.refs_1_, f32[128,256]{1,0:T(8,128)S(1)} %collective-permute-done.1.refs_2_, f32[128,256]{1,0:T(8,128)S(1)} %collective-permute-done.4.refs_3_, ...), custom_call_target="tpu_custom_call" | custom-call | bytes 1048576 | tf_op jit(solution)/shard_map/pallas_call | solution.py:174
  70.5 7.0 %all-to-all-start.2 = ((f32[16,128,256]{2,1,0:T(8,128)}), f32[16,128,256]{2,1,0:T(8,128)}, u32[]{:S(2)}, u32[]{:S(2)}) async-start(f32[16,128,256]{2,1,0:T(8,128)} %bitcast.13), calls=%async_computation.2 | async-start | bytes 4194304 | tf_op jit(solution)/shard_map/all_to_all | solution.py:321
  77.5 9.8 %shard_map.133 = (f32[8,128,256]{2,1,0:T(8,128)S(1)}, f32[8,128,256]{2,1,0:T(8,128)S(1)}) custom-call(f32[16,16,8,256]{3,2,1,0:T(8,128)S(1)} %all-to-all-done.1.panel_ref, bf16[2,2048,2048]{2,1,0:T(8,128)(2,1)} %shard_map.131.refs_9_.adj_ref), custom_call_target="tpu_custom_call" | custom-call | bytes 1048576 | tf_op jit(solution)/shard_map/pallas_call | solution.py:222
  87.7 2.4 %collective-permute-done.8 = f32[8,128,256]{2,1,0:T(8,128)S(1)} collective-permute-done((f32[8,128,256]{2,1,0:T(8,128)S(1)}, f32[8,128,256]{2,1,0:T(8,128)S(1)}, u32[]{:S(2)}, u32[]{:S(2)}) %collective-permute-start.8) | collective-permute-done | bytes 1048608 | tf_op jit(solution)/shard_map/ppermute | solution.py:261
  90.4 3.6 %collective-permute-start.10 = (f32[128,256]{1,0:T(8,128)S(1)}, f32[128,256]{1,0:T(8,128)S(1)}, u32[]{:S(2)}, u32[]{:S(2)}) collective-permute-start(f32[128,256]{1,0:T(8,128)S(1)} %get-tuple-element.37), channel_id=1, source_target_pairs={{0,14},{1,15},{2,0},{3,1},{4,2},{5,3},{6,4},{7,5},{8,6},{9,7},{10,... | collective-permute-start | bytes 393224 | tf_op jit(solution)/shard_map/ppermute | solution.py:257
  94.0 3.7 %collective-permute-done.9 = f32[128,256]{1,0:T(8,128)S(1)} collective-permute-done((f32[128,256]{1,0:T(8,128)S(1)}, f32[128,256]{1,0:T(8,128)S(1)}, u32[]{:S(2)}, u32[]{:S(2)}) %collective-permute-start.9) | collective-permute-done | bytes 131104 | tf_op jit(solution)/shard_map/ppermute | solution.py:257
  100.6 3.1 %collective-permute-done.11 = f32[128,256]{1,0:T(8,128)S(1)} collective-permute-done((f32[128,256]{1,0:T(8,128)S(1)}, f32[128,256]{1,0:T(8,128)S(1)}, u32[]{:S(2)}, u32[]{:S(2)}) %collective-permute-start.11) | collective-permute-done | bytes 131104 | tf_op jit(solution)/shard_map/ppermute | solution.py:257
  103.6 7.3 %all-to-all-done.2 = f32[16,128,256]{2,1,0:T(8,128)} async-done(((f32[16,128,256]{2,1,0:T(8,128)}), f32[16,128,256]{2,1,0:T(8,128)}, u32[]{:S(2)}, u32[]{:S(2)}) %all-to-all-start.2) | async-done | bytes 2097184 | tf_op jit(solution)/shard_map/all_to_all | solution.py:321
  111.1 3.9 %collective-permute-start.14 = (f32[128,256]{1,0:T(8,128)S(1)}, f32[128,256]{1,0:T(8,128)S(1)}, u32[]{:S(2)}, u32[]{:S(2)}) collective-permute-start(f32[128,256]{1,0:T(8,128)S(1)} %get-tuple-element.44), channel_id=1, source_target_pairs={{0,14},{1,15},{2,0},{3,1},{4,2},{5,3},{6,4},{7,5},{8,6},{9,7},{10,... | collective-permute-start | bytes 393224 | tf_op jit(solution)/shard_map/ppermute | solution.py:257
  114.9 1.7 %reduce_sum.11 = f32[128,256]{1,0:T(8,128)S(1)} reduce(f32[16,128,256]{2,1,0:T(8,128)} %all-to-all-done.2, f32[]{:T(128)} %constant.16.clone.1), dimensions={0}, to_apply=%region_0.0 | reduce | flops 491520 | bytes 2228228 | tf_op jit(solution)/shard_map/reduce_sum | solution.py:336
  119.2 3.6 %collective-permute-done.15 = f32[128,256]{1,0:T(8,128)S(1)} collective-permute-done((f32[128,256]{1,0:T(8,128)S(1)}, f32[128,256]{1,0:T(8,128)S(1)}, u32[]{:S(2)}, u32[]{:S(2)}) %collective-permute-start.15) | collective-permute-done | bytes 131104 | tf_op jit(solution)/shard_map/ppermute | solution.py:257
  (47 shorter events, 14.0 us)
Async XLA Ops:
  4.7 13.3 %collective-permute-start.2 = (f32[128,256]{1,0:T(8,128)S(1)}, f32[128,256]{1,0:T(8,128)S(1)}, u32[]{:S(2)}, u32[]{:S(2)}) collective-permute-start(f32[128,256]{1,0:T(8,128)S(1)} %maximum_multiply_fusion.refs_0_), channel_id=1, source_target_pairs={{0,2},{1,3},{2,4},{3,5},{4,6},{5,7},{6,8},{7,9},{8,10},{9,11},{10,... | collective-permute-start | bytes 393224 | tf_op jit(solution)/shard_map/ppermute | solution.py:257
  7.2 12.2 %collective-permute-start = (f32[128,256]{1,0:T(8,128)S(1)}, f32[128,256]{1,0:T(8,128)S(1)}, u32[]{:S(2)}, u32[]{:S(2)}) collective-permute-start(f32[128,256]{1,0:T(8,128)S(1)} %maximum_multiply_fusion.refs_0_), channel_id=1, source_target_pairs={{0,14},{1,15},{2,0},{3,1},{4,2},{5,3},{6,4},{7,5},{8,6},{9,7},{10,... | collective-permute-start | bytes 393224 | tf_op jit(solution)/shard_map/ppermute | solution.py:257
  11.3 19.3 %all-to-all-start = ((f32[16,17,128]{2,1,0:T(8,128)}), f32[16,17,128]{2,1,0:T(8,128)S(1)}, u32[]{:S(2)}, u32[]{:S(2)}) async-start(f32[16,17,128]{2,1,0:T(8,128)} %pad_maximum_fusion), calls=%async_computation | async-start | bytes 393216 | tf_op jit(solution)/shard_map/all_to_all | solution.py:292
  18.0 12.6 %collective-permute-start.3 = (f32[128,256]{1,0:T(8,128)S(1)}, f32[128,256]{1,0:T(8,128)S(1)}, u32[]{:S(2)}, u32[]{:S(2)}) collective-permute-start(f32[128,256]{1,0:T(8,128)S(1)} %collective-permute-done.2.refs_7_), channel_id=1, source_target_pairs={{0,2},{1,3},{2,4},{3,5},{4,6},{5,7},{6,8},{7,9},{8,10},{9,11},{10,... | collective-permute-start | bytes 393224 | tf_op jit(solution)/shard_map/ppermute | solution.py:257
  19.5 11.1 %collective-permute-start.1 = (f32[128,256]{1,0:T(8,128)S(1)}, f32[128,256]{1,0:T(8,128)S(1)}, u32[]{:S(2)}, u32[]{:S(2)}) collective-permute-start(f32[128,256]{1,0:T(8,128)S(1)} %collective-permute-done.refs_1_), channel_id=1, source_target_pairs={{0,14},{1,15},{2,0},{3,1},{4,2},{5,3},{6,4},{7,5},{8,6},{9,7},{10,... | collective-permute-start | bytes 393224 | tf_op jit(solution)/shard_map/ppermute | solution.py:257
  21.4 0.7 copy-start
  22.1 0.7 copy-start.2
  32.2 38.4 %all-to-all-start.1 = ((f32[16,16,8,256]{3,2,1,0:T(8,128)}), f32[16,16,8,256]{3,2,1,0:T(8,128)S(1)}, u32[]{:S(2)}, u32[]{:S(2)}) async-start(f32[16,16,8,256]{3,2,1,0:T(8,128)} %broadcast_in_dim.2), calls=%async_computation.1 | async-start | bytes 4194304 | tf_op jit(solution)/shard_map/all_to_all | solution.py:313
  38.9 11.8 %copy-start.1 = (s32[1,1,128]{2,1,0:T(1,128)S(1)}, s32[1,1,128]{2,1,0:T(1,128)}, u32[]{:S(2)}) copy-start(s32[1,1,128]{2,1,0:T(1,128)} %param.17) | copy-start | bytes 1540
  38.9 11.8 %copy-start.3 = (s32[1,1,128]{2,1,0:T(1,128)S(1)}, s32[1,1,128]{2,1,0:T(1,128)}, u32[]{:S(2)}) copy-start(s32[1,1,128]{2,1,0:T(1,128)} %param.18) | copy-start | bytes 1540
  39.0 3.9 %collective-permute-start.4 = (f32[128,256]{1,0:T(8,128)S(1)}, f32[128,256]{1,0:T(8,128)S(1)}, u32[]{:S(2)}, u32[]{:S(2)}) collective-permute-start(f32[128,256]{1,0:T(8,128)S(1)} %collective-permute-done.1.refs_2_), channel_id=1, source_target_pairs={{0,14},{1,15},{2,0},{3,1},{4,2},{5,3},{6,4},{7,5},{8,6},{9,7},{10,... | collective-permute-start | bytes 393224 | tf_op jit(solution)/shard_map/ppermute | solution.py:257
  40.5 5.3 %collective-permute-start.6 = (f32[128,256]{1,0:T(8,128)S(1)}, f32[128,256]{1,0:T(8,128)S(1)}, u32[]{:S(2)}, u32[]{:S(2)}) collective-permute-start(f32[128,256]{1,0:T(8,128)S(1)} %collective-permute-done.3.refs_6_), channel_id=1, source_target_pairs={{0,2},{1,3},{2,4},{3,5},{4,6},{5,7},{6,8},{7,9},{8,10},{9,11},{10,... | collective-permute-start | bytes 393224 | tf_op jit(solution)/shard_map/ppermute | solution.py:257
  42.9 4.6 %collective-permute-start.5 = (f32[128,256]{1,0:T(8,128)S(1)}, f32[128,256]{1,0:T(8,128)S(1)}, u32[]{:S(2)}, u32[]{:S(2)}) collective-permute-start(f32[128,256]{1,0:T(8,128)S(1)} %collective-permute-done.4.refs_3_), channel_id=1, source_target_pairs={{0,14},{1,15},{2,0},{3,1},{4,2},{5,3},{6,4},{7,5},{8,6},{9,7},{10,... | collective-permute-start | bytes 393224 | tf_op jit(solution)/shard_map/ppermute | solution.py:257
  47.6 11.0 %collective-permute-start.7 = (f32[8,128,256]{2,1,0:T(8,128)S(1)}, f32[8,128,256]{2,1,0:T(8,128)S(1)}, u32[]{:S(2)}, u32[]{:S(2)}) collective-permute-start(f32[8,128,256]{2,1,0:T(8,128)S(1)} %shard_map.130), channel_id=1, source_target_pairs={{0,1},{1,0},{2,3},{3,2},{4,5},{5,4},{6,7},{7,6},{8,9},{9,8},{10,11... | collective-permute-start | bytes 3145736 | tf_op jit(solution)/shard_map/ppermute | solution.py:261
  70.5 40.4 %all-to-all-start.2 = ((f32[16,128,256]{2,1,0:T(8,128)}), f32[16,128,256]{2,1,0:T(8,128)}, u32[]{:S(2)}, u32[]{:S(2)}) async-start(f32[16,128,256]{2,1,0:T(8,128)} %bitcast.13), calls=%async_computation.2 | async-start | bytes 4194304 | tf_op jit(solution)/shard_map/all_to_all | solution.py:321
  87.3 2.7 %collective-permute-start.8 = (f32[8,128,256]{2,1,0:T(8,128)S(1)}, f32[8,128,256]{2,1,0:T(8,128)S(1)}, u32[]{:S(2)}, u32[]{:S(2)}) collective-permute-start(f32[8,128,256]{2,1,0:T(8,128)S(1)} %get-tuple-element.35), channel_id=1, source_target_pairs={{0,1},{1,0},{2,3},{3,2},{4,5},{5,4},{6,7},{7,6},{8,9},{9,8},{10,11... | collective-permute-start | bytes 3145736 | tf_op jit(solution)/shard_map/ppermute | solution.py:261
  90.1 7.6 %collective-permute-start.9 = (f32[128,256]{1,0:T(8,128)S(1)}, f32[128,256]{1,0:T(8,128)S(1)}, u32[]{:S(2)}, u32[]{:S(2)}) collective-permute-start(f32[128,256]{1,0:T(8,128)S(1)} %get-tuple-element.36), channel_id=1, source_target_pairs={{0,2},{1,3},{2,4},{3,5},{4,6},{5,7},{6,8},{7,9},{8,10},{9,11},{10,... | collective-permute-start | bytes 393224 | tf_op jit(solution)/shard_map/ppermute | solution.py:257
  90.4 7.3 %collective-permute-start.10 = (f32[128,256]{1,0:T(8,128)S(1)}, f32[128,256]{1,0:T(8,128)S(1)}, u32[]{:S(2)}, u32[]{:S(2)}) collective-permute-start(f32[128,256]{1,0:T(8,128)S(1)} %get-tuple-element.37), channel_id=1, source_target_pairs={{0,14},{1,15},{2,0},{3,1},{4,2},{5,3},{6,4},{7,5},{8,6},{9,7},{10,... | collective-permute-start | bytes 393224 | tf_op jit(solution)/shard_map/ppermute | solution.py:257
  97.8 5.8 %collective-permute-start.11 = (f32[128,256]{1,0:T(8,128)S(1)}, f32[128,256]{1,0:T(8,128)S(1)}, u32[]{:S(2)}, u32[]{:S(2)}) collective-permute-start(f32[128,256]{1,0:T(8,128)S(1)} %get-tuple-element.38), channel_id=1, source_target_pairs={{0,2},{1,3},{2,4},{3,5},{4,6},{5,7},{6,8},{7,9},{8,10},{9,11},{10,... | collective-permute-start | bytes 393224 | tf_op jit(solution)/shard_map/ppermute | solution.py:257
  99.1 4.5 %collective-permute-start.12 = (f32[128,256]{1,0:T(8,128)S(1)}, f32[128,256]{1,0:T(8,128)S(1)}, u32[]{:S(2)}, u32[]{:S(2)}) collective-permute-start(f32[128,256]{1,0:T(8,128)S(1)} %get-tuple-element.39), channel_id=1, source_target_pairs={{0,14},{1,15},{2,0},{3,1},{4,2},{5,3},{6,4},{7,5},{8,6},{9,7},{10,... | collective-permute-start | bytes 393224 | tf_op jit(solution)/shard_map/ppermute | solution.py:257
  111.0 6.8 %collective-permute-start.13 = (f32[128,256]{1,0:T(8,128)S(1)}, f32[128,256]{1,0:T(8,128)S(1)}, u32[]{:S(2)}, u32[]{:S(2)}) collective-permute-start(f32[128,256]{1,0:T(8,128)S(1)} %get-tuple-element.43), channel_id=1, source_target_pairs={{0,2},{1,3},{2,4},{3,5},{4,6},{5,7},{6,8},{7,9},{8,10},{9,11},{10,... | collective-permute-start | bytes 393224 | tf_op jit(solution)/shard_map/ppermute | solution.py:257
  111.1 6.7 %collective-permute-start.14 = (f32[128,256]{1,0:T(8,128)S(1)}, f32[128,256]{1,0:T(8,128)S(1)}, u32[]{:S(2)}, u32[]{:S(2)}) collective-permute-start(f32[128,256]{1,0:T(8,128)S(1)} %get-tuple-element.44), channel_id=1, source_target_pairs={{0,14},{1,15},{2,0},{3,1},{4,2},{5,3},{6,4},{7,5},{8,6},{9,7},{10,... | collective-permute-start | bytes 393224 | tf_op jit(solution)/shard_map/ppermute | solution.py:257
  117.8 5.1 %collective-permute-start.15 = (f32[128,256]{1,0:T(8,128)S(1)}, f32[128,256]{1,0:T(8,128)S(1)}, u32[]{:S(2)}, u32[]{:S(2)}) collective-permute-start(f32[128,256]{1,0:T(8,128)S(1)} %fusion.1), channel_id=1, source_target_pairs={{0,2},{1,3},{2,4},{3,5},{4,6},{5,7},{6,8},{7,9},{8,10},{9,11},{10,... | collective-permute-start | bytes 393224 | tf_op jit(solution)/shard_map/ppermute | solution.py:257

commit v3 on v2

--- a/solution.py
+++ b/solution.py
@@ -15,6 +15,7 @@
 HALF = TILES // 2
 BLOCK = 256
 MIB = 1 << 20
+LATE = (True, 2)
 F32 = jnp.float32
 BF16 = jnp.bfloat16
 
@@ -140,8 +141,7 @@
     return finish, after
 
 
-def track_kernel(*refs):
-    blocks, (theirs_ref, adj_ref, out_ref, phi, plo, slots, sems) = refs[:8], refs[8:]
+def track_kernel(mine_ref, theirs_ref, adj_ref, out_ref, phi, plo, slots, sems):
     track = lax.axis_index("track")
     core = lax.rem(track, 2)
     finish, after = stream(adj_ref, slots, sems, lambda b: (slice(None), rows_of(b, BLOCK)))
@@ -152,10 +152,13 @@
         phi[:, at] = high
         plo[:, at] = low
 
-    for d in range(8):
+    def both(d, carry):
         z = lax.rem(lax.div(track, 2) + d, 8)
-        put(2 * z + core, blocks[d][...])
+        put(2 * z + core, mine_ref[d])
         put(2 * z + 1 - core, theirs_ref[d])
+        return carry
+
+    lax.fori_loop(0, 8, both, 0)
 
     def one(b, carry):
         at = rows_of(b, BLOCK)
@@ -170,10 +173,10 @@
     lax.fori_loop(0, BLOCKS, one, 0)
 
 
-def track_sums(blocks, theirs, adj):
+def track_sums(mine, theirs, adj):
     return pl.pallas_call(
         track_kernel,
-        in_specs=[VMEM] * 9 + [HBM],
+        in_specs=[VMEM, VMEM, HBM],
         out_specs=VMEM,
         scratch_shapes=[pltpu.VMEM((2 * EMB, SIZE), BF16)] * 2
         + [pltpu.VMEM((DEPTH, 2, SIZE, BLOCK), BF16)]
@@ -181,15 +184,17 @@
         out_shape=jax.ShapeDtypeStruct((SIZE, 2 * EMB), F32),
         compiler_params=pltpu.CompilerParams(vmem_limit_bytes=46 * MIB),
         cost_estimate=cost(MIB),
-    )(*blocks, theirs, adj)
-
-
-def user_kernel(panel_ref, adj_ref, keep_ref, send_ref, phi, plo, sums, slots, sems):
+    )(mine, theirs, adj)
+
+
+def user_kernel(panel_ref, adj_ref, keep_a, keep_b, send_a, send_b, phi, plo, sums, slots, sems):
     track = lax.axis_index("track")
     core = lax.rem(track, 2)
 
     def block(b):
-        return rows_of(lax.rem(lax.div(track, 2) + b, 8), BLOCK)
+        step = lax.div(b, 2)
+        ahead = jnp.where(lax.rem(b, 2) == 0, 4 - step, 5 + step)
+        return rows_of(lax.rem(lax.div(track, 2) + ahead, 8), BLOCK)
 
     finish, after = stream(adj_ref, slots, sems, lambda b: (block(b), slice(None)))
 
@@ -211,8 +216,17 @@
         out += jnp.dot(hi, plo[...], preferred_element_type=F32)
         sums[...] = out
         after(b)
-        keep_ref[b] = sums[rows_of(core, TILE), :]
-        send_ref[b] = sums[rows_of(1 - core, TILE), :]
+
+        @pl.when(b < 4)
+        def _():
+            keep_a[b] = sums[rows_of(core, TILE), :]
+            send_a[b] = sums[rows_of(1 - core, TILE), :]
+
+        @pl.when(b >= 4)
+        def _():
+            keep_b[b - 4] = sums[rows_of(core, TILE), :]
+            send_b[b - 4] = sums[rows_of(1 - core, TILE), :]
+
         return carry
 
     lax.fori_loop(0, BLOCKS, one, 0)
@@ -222,7 +236,7 @@
     return pl.pallas_call(
         user_kernel,
         in_specs=[VMEM, HBM],
-        out_specs=[VMEM] * 2,
+        out_specs=[VMEM] * 4,
         scratch_shapes=[
             pltpu.VMEM((SIZE, 2 * EMB), BF16),
             pltpu.VMEM((SIZE, 2 * EMB), BF16),
@@ -230,7 +244,7 @@
             pltpu.VMEM((DEPTH, 2, BLOCK, SIZE), BF16),
         ]
         + STREAM,
-        out_shape=[jax.ShapeDtypeStruct((8, TILE, 2 * EMB), F32)] * 2,
+        out_shape=[jax.ShapeDtypeStruct((4, TILE, 2 * EMB), F32)] * 4,
         compiler_params=pltpu.CompilerParams(vmem_limit_bytes=46 * MIB),
         cost_estimate=cost(MIB),
     )(panel, adj)
@@ -313,26 +327,27 @@
     panel = lax.all_to_all(
         jnp.broadcast_to(share, (TILES,) + share.shape), "user", split_axis=0, concat_axis=0
     )
-    theirs = swap_core(pack(blocks))
-    to_tracks = track_sums(blocks, theirs, adj)
+    mine = pack(blocks)
+    theirs = swap_core(mine)
+    to_tracks = track_sums(mine, theirs, adj)
     to_tracks, panel = lax.optimization_barrier((to_tracks, panel))
-    keep, send = user_sums(panel, adj)
+    keep_a, keep_b, send_a, send_b = user_sums(panel, adj)
     own_scale = lax.dynamic_slice_in_dim(scale_rows, user, 1, 0).reshape(TILE, 1)
     landed = lax.all_to_all(
         to_tracks.reshape(TILES, TILE, 2 * EMB), "user", split_axis=0, concat_axis=0, tiled=True
     )
-    got = swap_core(send)
-    up, down = lax.optimization_barrier((keep[4] + got[4], keep[5] + got[5]))
-    for d in (3, 2, 1):
+    got_a, got_b = swap_core(send_a), swap_core(send_b)
+    up, down = lax.optimization_barrier((keep_a[0] + got_a[0], keep_a[1] + got_a[1]))
+    for keep, got, d in ((keep_a, got_a, 2), (keep_b, got_b, 0), (keep_b, got_b, 2)):
         up, down = shift_z(up, 1), shift_z(down, -1)
-        if d == 2:
+        if LATE == (keep is keep_b, d):
             up, down, landed = lax.optimization_barrier((up, down, landed))
         up = up + (keep[d] + got[d])
-        if d > 1:
-            down = down + (keep[9 - d] + got[9 - d])
+        if keep is keep_a or d == 0:
+            down = down + (keep[d + 1] + got[d + 1])
         up, down = lax.optimization_barrier((up, down))
     up = shift_z(up, 1)
-    user_total = (keep[0] + got[0] + up + down) * user_scale[:, None]
+    user_total = (keep_b[3] + got_b[3] + up + down) * user_scale[:, None]
     track_total = (jnp.sum(landed, axis=0) * own_scale).reshape(1, 1, TILE, 2 * EMB)
     return (
         user_total[:, :EMB],

time: 124 us -> 117 us (0.944)
  waiting for transfers between devices: 25.4 us -> 20.4 us
  starting transfers between devices: 49 us -> 47.5 us
    all_to_all x1, waiting for transfers between devices: 7.31 us -> 3.09 us  [body(): lax.all_to_all(to_tracks.reshape(TILES, TILE, 2 * EMB), 'user', split_axi...]
    ppermute x14, starting transfers between devices: 25 us -> 22.9 us  [shift_z(): return lax.ppermute(x, 'track', pairs)]
    ppermute x2 -> x3, starting transfers between devices: 3.54 us -> 4.08 us  [swap_core(): return lax.ppermute(x, 'track', [(t, t ^ 1) for t in range(16)])]
  transfers between devices with their start and end apart: 19 -> 20, of which waited for: 9 -> 10; matrix products, arithmetic and copies ran while one was open for 2% -> 2% of each run, Pallas kernels for 30% -> 32%
where the time goes in v3:
time: 117 us; the launch traced here: 116 us
  starting transfers between devices  47.5 us (41%)
  Pallas kernels  36.7 us (31%)
  waiting for transfers between devices  20.4 us (17%)
  other arithmetic  6.03 us (5%)
  local copies, waits for them, and re-layouts  4.28 us (4%)
  between operations  1.5 us (1%)
    ppermute x14, starting transfers between devices, shift_z(): return lax.ppermute(x, 'track', pairs)  22.9 us
    ppermute x14, waiting for transfers between devices, shift_z(): return lax.ppermute(x, 'track', pairs)  15.9 us
    pallas_call x2, Pallas kernels, build(): pl.pallas_call(functools.partial(build_kernel, half), in_specs=[SMEM, SME...  15.6 us
    pallas_call x1, Pallas kernels, track_sums(): pl.pallas_call(track_kernel, in_specs=[VMEM, VMEM, HBM], out_specs=VMEM,...  11.3 us
    pallas_call x1, Pallas kernels, user_sums(): pl.pallas_call(user_kernel, in_specs=[VMEM, HBM], out_specs=[VMEM] * 4, s...  9.69 us
    all_to_all x1, starting transfers between devices, body(): lax.all_to_all(to_tracks.reshape(TILES, TILE, 2 * EMB), 'user', split_axi...  7 us
    all_to_all x1, starting transfers between devices, body(): lax.all_to_all(jnp.broadcast_to(share, (TILES,) + share.shape), 'user', s...  6.75 us
    all_to_all x1, starting transfers between devices, body(): lax.all_to_all(moving, 'track', split_axis=0, concat_axis=0, tiled=True)  6.72 us
  transfers between devices with their start and end apart: 20, of which 10 were waited for; matrix products, arithmetic and copies ran while one was open for 2% of the time, Pallas kernels for 32%

profile of v3, /device:TPU:1, one launch (start us, length us, event | category | flops | bytes accessed | tf_op | source)
XLA Modules:
  0.0 116.4 jit_solution(11855525772991149456)
XLA Ops:
  4.7 2.5 %collective-permute-start.2 = (f32[128,256]{1,0:T(8,128)S(1)}, f32[128,256]{1,0:T(8,128)S(1)}, u32[]{:S(2)}, u32[]{:S(2)}) collective-permute-start(f32[128,256]{1,0:T(8,128)S(1)} %maximum_multiply_fusion.refs_0_), channel_id=1, source_target_pairs={{0,2},{1,3},{2,4},{3,5},{4,6},{5,7},{6,8},{7,9},{8,10},{9,11},{10,... | collective-permute-start | bytes 393224 | tf_op jit(solution)/shard_map/ppermute | solution.py:271
  7.2 4.0 %collective-permute-start = (f32[128,256]{1,0:T(8,128)S(1)}, f32[128,256]{1,0:T(8,128)S(1)}, u32[]{:S(2)}, u32[]{:S(2)}) collective-permute-start(f32[128,256]{1,0:T(8,128)S(1)} %maximum_multiply_fusion.refs_0_), channel_id=1, source_target_pairs={{0,14},{1,15},{2,0},{3,1},{4,2},{5,3},{6,4},{7,5},{8,6},{9,7},{10,... | collective-permute-start | bytes 393224 | tf_op jit(solution)/shard_map/ppermute | solution.py:271
  11.3 6.7 %all-to-all-start = ((f32[16,17,128]{2,1,0:T(8,128)}), f32[16,17,128]{2,1,0:T(8,128)S(1)}, u32[]{:S(2)}, u32[]{:S(2)}) async-start(f32[16,17,128]{2,1,0:T(8,128)} %pad_maximum_fusion), calls=%async_computation | async-start | bytes 393216 | tf_op jit(solution)/shard_map/all_to_all | solution.py:306
  18.0 1.5 %collective-permute-start.3 = (f32[128,256]{1,0:T(8,128)S(1)}, f32[128,256]{1,0:T(8,128)S(1)}, u32[]{:S(2)}, u32[]{:S(2)}) collective-permute-start(f32[128,256]{1,0:T(8,128)S(1)} %collective-permute-done.2.refs_7_), channel_id=1, source_target_pairs={{0,2},{1,3},{2,4},{3,5},{4,6},{5,7},{6,8},{7,9},{8,10},{9,11},{10,... | collective-permute-start | bytes 393224 | tf_op jit(solution)/shard_map/ppermute | solution.py:271
  22.7 7.8 %shard_map.129.refs_0_ = bf16[2,2048,2048]{2,1,0:T(8,128)(2,1)} custom-call(s32[128]{0:T(128)S(1)} %bitcast.48, s32[128]{0:T(128)S(1)} %bitcast.50, s32[1]{0:T(128)} %bitcast.46.count_ref, f32[128,128,128]{2,1,0:T(8,128)} %bitcast.52), custom_call_target="tpu_custom_call" | custom-call | tf_op jit(solution)/shard_map/pallas_call | solution.py:97
  30.6 1.6 %broadcast_in_dim.2 = f32[16,16,8,256]{3,2,1,0:T(8,128)} broadcast(f32[16,8,256]{2,1,0:T(8,128)S(1)} %pad_maximum_fusion.1), dimensions={1,2,3} | broadcast | bytes 2228224 | tf_op jit(solution)/shard_map/broadcast_in_dim | solution.py:328
  32.2 6.8 %all-to-all-start.1 = ((f32[16,16,8,256]{3,2,1,0:T(8,128)}), f32[16,16,8,256]{3,2,1,0:T(8,128)S(1)}, u32[]{:S(2)}, u32[]{:S(2)}) async-start(f32[16,16,8,256]{3,2,1,0:T(8,128)} %broadcast_in_dim.2), calls=%async_computation.1 | async-start | bytes 4194304 | tf_op jit(solution)/shard_map/all_to_all | solution.py:327
  40.5 2.4 %collective-permute-done.4.refs_3_ = f32[128,256]{1,0:T(8,128)S(1)} collective-permute-done((f32[128,256]{1,0:T(8,128)S(1)}, f32[128,256]{1,0:T(8,128)S(1)}, u32[]{:S(2)}, u32[]{:S(2)}) %collective-permute-start.4) | collective-permute-done | bytes 131104 | tf_op jit(solution)/shard_map/ppermute | solution.py:271
  42.8 2.6 %collective-permute-start.5 = (f32[128,256]{1,0:T(8,128)S(1)}, f32[128,256]{1,0:T(8,128)S(1)}, u32[]{:S(2)}, u32[]{:S(2)}) collective-permute-start(f32[128,256]{1,0:T(8,128)S(1)} %collective-permute-done.4.refs_3_), channel_id=1, source_target_pairs={{0,14},{1,15},{2,0},{3,1},{4,2},{5,3},{6,4},{7,5},{8,6},{9,7},{10,... | collective-permute-start | bytes 393224 | tf_op jit(solution)/shard_map/ppermute | solution.py:271
  45.7 1.7 %collective-permute-done.5.refs_4_ = f32[128,256]{1,0:T(8,128)S(1)} collective-permute-done((f32[128,256]{1,0:T(8,128)S(1)}, f32[128,256]{1,0:T(8,128)S(1)}, u32[]{:S(2)}, u32[]{:S(2)}) %collective-permute-start.5) | collective-permute-done | bytes 131104 | tf_op jit(solution)/shard_map/ppermute | solution.py:271
  47.4 3.5 %collective-permute-start.7 = (f32[8,128,256]{2,1,0:T(8,128)S(1)}, f32[8,128,256]{2,1,0:T(8,128)S(1)}, u32[]{:S(2)}, u32[]{:S(2)}) collective-permute-start(f32[8,128,256]{2,1,0:T(8,128)S(1)} %shard_map.130.mine_ref), channel_id=1, source_target_pairs={{0,1},{1,0},{2,3},{3,2},{4,5},{5,4},{6,7},{7,6},{8,9},{9,8},{10,11... | collective-permute-start | bytes 3145736 | tf_op jit(solution)/shard_map/ppermute | solution.py:275
  50.9 7.8 %shard_map.131.adj_ref = bf16[2,2048,2048]{2,1,0:T(8,128)(2,1)} custom-call(s32[128]{0:T(128)S(1)} %bitcast.49, s32[128]{0:T(128)S(1)} %bitcast.51, s32[1]{0:T(128)} %bitcast.47.count_ref, f32[128,128,128]{2,1,0:T(8,128)} %bitcast.53, bf16[2,2048,2048]{2,1,0:T(8,128)(2,1)} %shard_map.129.refs_0_), custom_call_target="tpu_custom_call", output_to_operand_aliasing={{}: (4, {})} | custom-call | bytes 12582912 | tf_op jit(solution)/shard_map/pallas_call | solution.py:97
  58.8 11.3 %shard_map.132 = f32[2048,256]{1,0:T(8,128)} custom-call(f32[8,128,256]{2,1,0:T(8,128)S(1)} %shard_map.130.mine_ref, f32[8,128,256]{2,1,0:T(8,128)S(1)} %collective-permute-done.7.theirs_ref, bf16[2,2048,2048]{2,1,0:T(8,128)(2,1)} %shard_map.131.adj_ref), custom_call_target="tpu_custom_call" | custom-call | bytes 1048576 | tf_op jit(solution)/shard_map/pallas_call | solution.py:177
  70.1 7.0 %all-to-all-start.2 = ((f32[16,128,256]{2,1,0:T(8,128)}), f32[16,128,256]{2,1,0:T(8,128)}, u32[]{:S(2)}, u32[]{:S(2)}) async-start(f32[16,128,256]{2,1,0:T(8,128)} %bitcast.15), calls=%async_computation.2 | async-start | bytes 4194304 | tf_op jit(solution)/shard_map/all_to_all | solution.py:336
  77.1 9.7 %shard_map.133 = (f32[4,128,256]{2,1,0:T(8,128)S(1)}, f32[4,128,256]{2,1,0:T(8,128)S(1)}, f32[4,128,256]{2,1,0:T(8,128)S(1)}, f32[4,128,256]{2,1,0:T(8,128)S(1)}) custom-call(f32[16,16,8,256]{3,2,1,0:T(8,128)S(1)} %all-to-all-done.1.panel_ref, bf16[2,2048,2048]{2,1,0:T(8,128)(2,1)} %shard_map.131.adj_ref), custom_call_target="tpu_custom_call" | custom-call | bytes 1048576 | tf_op jit(solution)/shard_map/pallas_call | solution.py:236
  89.1 3.6 %collective-permute-start.11 = (f32[128,256]{1,0:T(8,128)S(1)}, f32[128,256]{1,0:T(8,128)S(1)}, u32[]{:S(2)}, u32[]{:S(2)}) collective-permute-start(f32[128,256]{1,0:T(8,128)S(1)} %get-tuple-element.41), channel_id=1, source_target_pairs={{0,14},{1,15},{2,0},{3,1},{4,2},{5,3},{6,4},{7,5},{8,6},{9,7},{10,... | collective-permute-start | bytes 393224 | tf_op jit(solution)/shard_map/ppermute | solution.py:271
  92.7 3.6 %collective-permute-done.10 = f32[128,256]{1,0:T(8,128)S(1)} collective-permute-done((f32[128,256]{1,0:T(8,128)S(1)}, f32[128,256]{1,0:T(8,128)S(1)}, u32[]{:S(2)}, u32[]{:S(2)}) %collective-permute-start.10) | collective-permute-done | bytes 131104 | tf_op jit(solution)/shard_map/ppermute | solution.py:271
  96.3 1.6 %collective-permute-start.12 = (f32[128,256]{1,0:T(8,128)S(1)}, f32[128,256]{1,0:T(8,128)S(1)}, u32[]{:S(2)}, u32[]{:S(2)}) collective-permute-start(f32[128,256]{1,0:T(8,128)S(1)} %get-tuple-element.42), channel_id=1, source_target_pairs={{0,2},{1,3},{2,4},{3,5},{4,6},{5,7},{6,8},{7,9},{8,10},{9,11},{10,... | collective-permute-start | bytes 393224 | tf_op jit(solution)/shard_map/ppermute | solution.py:271
  99.1 2.9 %collective-permute-done.12 = f32[128,256]{1,0:T(8,128)S(1)} collective-permute-done((f32[128,256]{1,0:T(8,128)S(1)}, f32[128,256]{1,0:T(8,128)S(1)}, u32[]{:S(2)}, u32[]{:S(2)}) %collective-permute-start.12) | collective-permute-done | bytes 131104 | tf_op jit(solution)/shard_map/ppermute | solution.py:271
  103.5 1.5 %collective-permute-start.15 = (f32[128,256]{1,0:T(8,128)S(1)}, f32[128,256]{1,0:T(8,128)S(1)}, u32[]{:S(2)}, u32[]{:S(2)}) collective-permute-start(f32[128,256]{1,0:T(8,128)S(1)} %get-tuple-element.45), channel_id=1, source_target_pairs={{0,14},{1,15},{2,0},{3,1},{4,2},{5,3},{6,4},{7,5},{8,6},{9,7},{10,... | collective-permute-start | bytes 393224 | tf_op jit(solution)/shard_map/ppermute | solution.py:271
  105.0 2.3 %collective-permute-done.14 = f32[128,256]{1,0:T(8,128)S(1)} collective-permute-done((f32[128,256]{1,0:T(8,128)S(1)}, f32[128,256]{1,0:T(8,128)S(1)}, u32[]{:S(2)}, u32[]{:S(2)}) %collective-permute-start.14) | collective-permute-done | bytes 131104 | tf_op jit(solution)/shard_map/ppermute | solution.py:271
  107.4 3.1 %all-to-all-done.2 = f32[16,128,256]{2,1,0:T(8,128)} async-done(((f32[16,128,256]{2,1,0:T(8,128)}), f32[16,128,256]{2,1,0:T(8,128)}, u32[]{:S(2)}, u32[]{:S(2)}) %all-to-all-start.2) | async-done | bytes 2097184 | tf_op jit(solution)/shard_map/all_to_all | solution.py:336
  110.6 1.7 %reduce_sum.11 = f32[128,256]{1,0:T(8,128)S(1)} reduce(f32[16,128,256]{2,1,0:T(8,128)} %all-to-all-done.2, f32[]{:T(128)} %constant.16.clone.1), dimensions={0}, to_apply=%region_0.0 | reduce | flops 491520 | bytes 2228228 | tf_op jit(solution)/shard_map/reduce_sum | solution.py:351
  113.1 2.6 %collective-permute-done.16 = f32[128,256]{1,0:T(8,128)S(1)} collective-permute-done((f32[128,256]{1,0:T(8,128)S(1)}, f32[128,256]{1,0:T(8,128)S(1)}, u32[]{:S(2)}, u32[]{:S(2)}) %collective-permute-start.16) | collective-permute-done | bytes 131104 | tf_op jit(solution)/shard_map/ppermute | solution.py:271
  (49 shorter events, 15.2 us)
Async XLA Ops:
  4.7 13.3 %collective-permute-start.2 = (f32[128,256]{1,0:T(8,128)S(1)}, f32[128,256]{1,0:T(8,128)S(1)}, u32[]{:S(2)}, u32[]{:S(2)}) collective-permute-start(f32[128,256]{1,0:T(8,128)S(1)} %maximum_multiply_fusion.refs_0_), channel_id=1, source_target_pairs={{0,2},{1,3},{2,4},{3,5},{4,6},{5,7},{6,8},{7,9},{8,10},{9,11},{10,... | collective-permute-start | bytes 393224 | tf_op jit(solution)/shard_map/ppermute | solution.py:271
  7.2 12.2 %collective-permute-start = (f32[128,256]{1,0:T(8,128)S(1)}, f32[128,256]{1,0:T(8,128)S(1)}, u32[]{:S(2)}, u32[]{:S(2)}) collective-permute-start(f32[128,256]{1,0:T(8,128)S(1)} %maximum_multiply_fusion.refs_0_), channel_id=1, source_target_pairs={{0,14},{1,15},{2,0},{3,1},{4,2},{5,3},{6,4},{7,5},{8,6},{9,7},{10,... | collective-permute-start | bytes 393224 | tf_op jit(solution)/shard_map/ppermute | solution.py:271
  11.3 19.3 %all-to-all-start = ((f32[16,17,128]{2,1,0:T(8,128)}), f32[16,17,128]{2,1,0:T(8,128)S(1)}, u32[]{:S(2)}, u32[]{:S(2)}) async-start(f32[16,17,128]{2,1,0:T(8,128)} %pad_maximum_fusion), calls=%async_computation | async-start | bytes 393216 | tf_op jit(solution)/shard_map/all_to_all | solution.py:306
  18.0 12.6 %collective-permute-start.3 = (f32[128,256]{1,0:T(8,128)S(1)}, f32[128,256]{1,0:T(8,128)S(1)}, u32[]{:S(2)}, u32[]{:S(2)}) collective-permute-start(f32[128,256]{1,0:T(8,128)S(1)} %collective-permute-done.2.refs_7_), channel_id=1, source_target_pairs={{0,2},{1,3},{2,4},{3,5},{4,6},{5,7},{6,8},{7,9},{8,10},{9,11},{10,... | collective-permute-start | bytes 393224 | tf_op jit(solution)/shard_map/ppermute | solution.py:271
  19.5 11.1 %collective-permute-start.1 = (f32[128,256]{1,0:T(8,128)S(1)}, f32[128,256]{1,0:T(8,128)S(1)}, u32[]{:S(2)}, u32[]{:S(2)}) collective-permute-start(f32[128,256]{1,0:T(8,128)S(1)} %collective-permute-done.refs_1_), channel_id=1, source_target_pairs={{0,14},{1,15},{2,0},{3,1},{4,2},{5,3},{6,4},{7,5},{8,6},{9,7},{10,... | collective-permute-start | bytes 393224 | tf_op jit(solution)/shard_map/ppermute | solution.py:271
  21.4 0.7 copy-start
  22.1 0.7 copy-start.2
  32.2 37.9 %all-to-all-start.1 = ((f32[16,16,8,256]{3,2,1,0:T(8,128)}), f32[16,16,8,256]{3,2,1,0:T(8,128)S(1)}, u32[]{:S(2)}, u32[]{:S(2)}) async-start(f32[16,16,8,256]{3,2,1,0:T(8,128)} %broadcast_in_dim.2), calls=%async_computation.1 | async-start | bytes 4194304 | tf_op jit(solution)/shard_map/all_to_all | solution.py:327
  38.9 12.0 %copy-start.1 = (s32[1,1,128]{2,1,0:T(1,128)S(1)}, s32[1,1,128]{2,1,0:T(1,128)}, u32[]{:S(2)}) copy-start(s32[1,1,128]{2,1,0:T(1,128)} %param.17) | copy-start | bytes 1540
  38.9 12.0 %copy-start.3 = (s32[1,1,128]{2,1,0:T(1,128)S(1)}, s32[1,1,128]{2,1,0:T(1,128)}, u32[]{:S(2)}) copy-start(s32[1,1,128]{2,1,0:T(1,128)} %param.18) | copy-start | bytes 1540
  38.9 3.9 %collective-permute-start.4 = (f32[128,256]{1,0:T(8,128)S(1)}, f32[128,256]{1,0:T(8,128)S(1)}, u32[]{:S(2)}, u32[]{:S(2)}) collective-permute-start(f32[128,256]{1,0:T(8,128)S(1)} %collective-permute-done.1.refs_2_), channel_id=1, source_target_pairs={{0,14},{1,15},{2,0},{3,1},{4,2},{5,3},{6,4},{7,5},{8,6},{9,7},{10,... | collective-permute-start | bytes 393224 | tf_op jit(solution)/shard_map/ppermute | solution.py:271
  40.4 5.3 %collective-permute-start.6 = (f32[128,256]{1,0:T(8,128)S(1)}, f32[128,256]{1,0:T(8,128)S(1)}, u32[]{:S(2)}, u32[]{:S(2)}) collective-permute-start(f32[128,256]{1,0:T(8,128)S(1)} %collective-permute-done.3.refs_6_), channel_id=1, source_target_pairs={{0,2},{1,3},{2,4},{3,5},{4,6},{5,7},{6,8},{7,9},{8,10},{9,11},{10,... | collective-permute-start | bytes 393224 | tf_op jit(solution)/shard_map/ppermute | solution.py:271
  42.8 4.5 %collective-permute-start.5 = (f32[128,256]{1,0:T(8,128)S(1)}, f32[128,256]{1,0:T(8,128)S(1)}, u32[]{:S(2)}, u32[]{:S(2)}) collective-permute-start(f32[128,256]{1,0:T(8,128)S(1)} %collective-permute-done.4.refs_3_), channel_id=1, source_target_pairs={{0,14},{1,15},{2,0},{3,1},{4,2},{5,3},{6,4},{7,5},{8,6},{9,7},{10,... | collective-permute-start | bytes 393224 | tf_op jit(solution)/shard_map/ppermute | solution.py:271
  47.4 11.3 %collective-permute-start.7 = (f32[8,128,256]{2,1,0:T(8,128)S(1)}, f32[8,128,256]{2,1,0:T(8,128)S(1)}, u32[]{:S(2)}, u32[]{:S(2)}) collective-permute-start(f32[8,128,256]{2,1,0:T(8,128)S(1)} %shard_map.130.mine_ref), channel_id=1, source_target_pairs={{0,1},{1,0},{2,3},{3,2},{4,5},{5,4},{6,7},{7,6},{8,9},{9,8},{10,11... | collective-permute-start | bytes 3145736 | tf_op jit(solution)/shard_map/ppermute | solution.py:275
  70.1 40.4 %all-to-all-start.2 = ((f32[16,128,256]{2,1,0:T(8,128)}), f32[16,128,256]{2,1,0:T(8,128)}, u32[]{:S(2)}, u32[]{:S(2)}) async-start(f32[16,128,256]{2,1,0:T(8,128)} %bitcast.15), calls=%async_computation.2 | async-start | bytes 4194304 | tf_op jit(solution)/shard_map/all_to_all | solution.py:336
  86.8 2.0 %collective-permute-start.9 = (f32[4,128,256]{2,1,0:T(8,128)S(1)}, f32[4,128,256]{2,1,0:T(8,128)S(1)}, u32[]{:S(2)}, u32[]{:S(2)}) collective-permute-start(f32[4,128,256]{2,1,0:T(8,128)S(1)} %get-tuple-element.39), channel_id=1, source_target_pairs={{0,1},{1,0},{2,3},{3,2},{4,5},{5,4},{6,7},{7,6},{8,9},{9,8},{10,11... | collective-permute-start | bytes 1572872 | tf_op jit(solution)/shard_map/ppermute | solution.py:275
  87.2 11.9 %collective-permute-start.8 = (f32[4,128,256]{2,1,0:T(8,128)S(1)}, f32[4,128,256]{2,1,0:T(8,128)S(1)}, u32[]{:S(2)}, u32[]{:S(2)}) collective-permute-start(f32[4,128,256]{2,1,0:T(8,128)S(1)} %get-tuple-element.37), channel_id=1, source_target_pairs={{0,1},{1,0},{2,3},{3,2},{4,5},{5,4},{6,7},{7,6},{8,9},{9,8},{10,11... | collective-permute-start | bytes 1572872 | tf_op jit(solution)/shard_map/ppermute | solution.py:275
  88.8 7.5 %collective-permute-start.10 = (f32[128,256]{1,0:T(8,128)S(1)}, f32[128,256]{1,0:T(8,128)S(1)}, u32[]{:S(2)}, u32[]{:S(2)}) collective-permute-start(f32[128,256]{1,0:T(8,128)S(1)} %get-tuple-element.40), channel_id=1, source_target_pairs={{0,2},{1,3},{2,4},{3,5},{4,6},{5,7},{6,8},{7,9},{8,10},{9,11},{10,... | collective-permute-start | bytes 393224 | tf_op jit(solution)/shard_map/ppermute | solution.py:271
  89.1 7.2 %collective-permute-start.11 = (f32[128,256]{1,0:T(8,128)S(1)}, f32[128,256]{1,0:T(8,128)S(1)}, u32[]{:S(2)}, u32[]{:S(2)}) collective-permute-start(f32[128,256]{1,0:T(8,128)S(1)} %get-tuple-element.41), channel_id=1, source_target_pairs={{0,14},{1,15},{2,0},{3,1},{4,2},{5,3},{6,4},{7,5},{8,6},{9,7},{10,... | collective-permute-start | bytes 393224 | tf_op jit(solution)/shard_map/ppermute | solution.py:271
  96.3 5.6 %collective-permute-start.12 = (f32[128,256]{1,0:T(8,128)S(1)}, f32[128,256]{1,0:T(8,128)S(1)}, u32[]{:S(2)}, u32[]{:S(2)}) collective-permute-start(f32[128,256]{1,0:T(8,128)S(1)} %get-tuple-element.42), channel_id=1, source_target_pairs={{0,2},{1,3},{2,4},{3,5},{4,6},{5,7},{6,8},{7,9},{8,10},{9,11},{10,... | collective-permute-start | bytes 393224 | tf_op jit(solution)/shard_map/ppermute | solution.py:271
  98.0 4.2 %collective-permute-start.13 = (f32[128,256]{1,0:T(8,128)S(1)}, f32[128,256]{1,0:T(8,128)S(1)}, u32[]{:S(2)}, u32[]{:S(2)}) collective-permute-start(f32[128,256]{1,0:T(8,128)S(1)} %get-tuple-element.43), channel_id=1, source_target_pairs={{0,14},{1,15},{2,0},{3,1},{4,2},{5,3},{6,4},{7,5},{8,6},{9,7},{10,... | collective-permute-start | bytes 393224 | tf_op jit(solution)/shard_map/ppermute | solution.py:271
  102.3 5.1 %collective-permute-start.14 = (f32[128,256]{1,0:T(8,128)S(1)}, f32[128,256]{1,0:T(8,128)S(1)}, u32[]{:S(2)}, u32[]{:S(2)}) collective-permute-start(f32[128,256]{1,0:T(8,128)S(1)} %get-tuple-element.44), channel_id=1, source_target_pairs={{0,2},{1,3},{2,4},{3,5},{4,6},{5,7},{6,8},{7,9},{8,10},{9,11},{10,... | collective-permute-start | bytes 393224 | tf_op jit(solution)/shard_map/ppermute | solution.py:271
  103.5 3.9 %collective-permute-start.15 = (f32[128,256]{1,0:T(8,128)S(1)}, f32[128,256]{1,0:T(8,128)S(1)}, u32[]{:S(2)}, u32[]{:S(2)}) collective-permute-start(f32[128,256]{1,0:T(8,128)S(1)} %get-tuple-element.45), channel_id=1, source_target_pairs={{0,14},{1,15},{2,0},{3,1},{4,2},{5,3},{6,4},{7,5},{8,6},{9,7},{10,... | collective-permute-start | bytes 393224 | tf_op jit(solution)/shard_map/ppermute | solution.py:271
  110.5 5.1 %collective-permute-start.16 = (f32[128,256]{1,0:T(8,128)S(1)}, f32[128,256]{1,0:T(8,128)S(1)}, u32[]{:S(2)}, u32[]{:S(2)}) collective-permute-start(f32[128,256]{1,0:T(8,128)S(1)} %fusion.1), channel_id=1, source_target_pairs={{0,2},{1,3},{2,4},{3,5},{4,6},{5,7},{6,8},{7,9},{8,10},{9,11},{10,... | collective-permute-start | bytes 393224 | tf_op jit(solution)/shard_map/ppermute | solution.py:271

commit v4 on v3

--- a/solution.py
+++ b/solution.py
@@ -11,7 +11,6 @@
 TILES = 16
 EMB = 128
 SLOTS = 128
-SLOT_STEP = 16
 HALF = TILES // 2
 BLOCK = 256
 MIB = 1 << 20
@@ -31,32 +30,34 @@
 
 def build_kernel(half, row_ref, col_ref, count_ref, vals_ref, *refs):
     out_ref, slots, dense, hi, lo, sems = refs[-6:]
-    loads = SLOTS // SLOT_STEP
-    copies = []
-    for i in range(loads):
-        part = pl.ds(i * SLOT_STEP, SLOT_STEP)
-        copies.append(pltpu.make_async_copy(vals_ref.at[part], slots.at[part], sems.at[i]))
-        copies[-1].start()
+
+    def load(s):
+        return pltpu.make_async_copy(vals_ref.at[s], slots.at[s], sems.at[s])
+
+    def if_mine(s, do):
+        row = row_ref[s] - half * HALF
+        pl.when((row >= 0) & (row < HALF))(lambda: do(row))
+
+    def fetch(s, carry):
+        if_mine(s, lambda row: load(s).start())
+        return carry
 
     def clear(i, carry):
         dense[i] = jnp.zeros((TILE, TILE), F32)
         return carry
 
+    def add(s, carry):
+        def do(row):
+            load(s).wait()
+            dense[row * TILES + col_ref[s]] += slots[s]
+
+        if_mine(s, do)
+        return carry
+
+    live = jnp.clip(count_ref[0], 0, SLOTS)
+    lax.fori_loop(0, live, fetch, 0)
     lax.fori_loop(0, HALF * TILES, clear, 0)
-
-    def add(s, carry):
-        row = row_ref[s] - half * HALF
-
-        @pl.when((row >= 0) & (row < HALF))
-        def _():
-            dense[row * TILES + col_ref[s]] += slots[s]
-
-        return carry
-
-    for i in range(loads):
-        copies[i].wait()
-        live = jnp.clip(count_ref[0], i * SLOT_STEP, (i + 1) * SLOT_STEP)
-        lax.fori_loop(i * SLOT_STEP, live, add, 0)
+    lax.fori_loop(0, live, add, 0)
 
     copies = []
     for b in range(HALF // 2):
@@ -105,7 +106,7 @@
             pltpu.VMEM((HALF * TILES, TILE, TILE), F32),
             pltpu.VMEM((HALF * TILE, SIZE), BF16),
             pltpu.VMEM((HALF * TILE, SIZE), BF16),
-            pltpu.SemaphoreType.DMA((SLOTS // SLOT_STEP,)),
+            pltpu.SemaphoreType.DMA((SLOTS,)),
         ],
         compiler_params=pltpu.CompilerParams(vmem_limit_bytes=46 * MIB),
         cost_estimate=cost(12 * MIB * half),

time: 117 us -> 120 us (1.026)
  starting transfers between devices: 47.5 us -> 50.1 us
  waiting for transfers between devices: 20.4 us -> 22.4 us
    ppermute x14, waiting for transfers between devices: 15.9 us -> 19.4 us  [shift_z(): return lax.ppermute(x, 'track', pairs)]
    all_to_all x1, starting transfers between devices: 6.75 us -> 8.4 us  [body(): lax.all_to_all(jnp.broadcast_to(share, (TILES,) + share.shape), 'user', s...]
    all_to_all x1, waiting for transfers between devices: 3.09 us -> 1.54 us  [body(): lax.all_to_all(to_tracks.reshape(TILES, TILE, 2 * EMB), 'user', split_axi...]
    ppermute x3, starting transfers between devices: 4.08 us -> 2.85 us  [swap_core(): return lax.ppermute(x, 'track', [(t, t ^ 1) for t in range(16)])]
    ppermute x14, starting transfers between devices: 22.9 us -> 24.2 us  [shift_z(): return lax.ppermute(x, 'track', pairs)]
  transfers between devices with their start and end apart: 20 -> 20, of which waited for: 10 -> 10; matrix products, arithmetic and copies ran while one was open for 2% -> 2% of each run, Pallas kernels for 32% -> 30%
where the time goes in v4:
time: 120 us
  starting transfers between devices  50.1 us (42%)
  Pallas kernels  35.9 us (30%)
  waiting for transfers between devices  22.4 us (19%)
  other arithmetic  6.02 us (5%)
  local copies, waits for them, and re-layouts  4.28 us (4%)
  between operations  1.48 us (1%)
    ppermute x14, starting transfers between devices, shift_z(): return lax.ppermute(x, 'track', pairs)  24.2 us
    ppermute x14, waiting for transfers between devices, shift_z(): return lax.ppermute(x, 'track', pairs)  19.4 us
    pallas_call x2, Pallas kernels, build(): pl.pallas_call(functools.partial(build_kernel, half), in_specs=[SMEM, SME...  14.9 us
    pallas_call x1, Pallas kernels, track_sums(): pl.pallas_call(track_kernel, in_specs=[VMEM, VMEM, HBM], out_specs=VMEM,...  11.3 us
    pallas_call x1, Pallas kernels, user_sums(): pl.pallas_call(user_kernel, in_specs=[VMEM, HBM], out_specs=[VMEM] * 4, s...  9.69 us
    all_to_all x1, starting transfers between devices, body(): lax.all_to_all(jnp.broadcast_to(share, (TILES,) + share.shape), 'user', s...  8.4 us
    all_to_all x1, starting transfers between devices, body(): lax.all_to_all(to_tracks.reshape(TILES, TILE, 2 * EMB), 'user', split_axi...  8 us
    all_to_all x1, starting transfers between devices, body(): lax.all_to_all(moving, 'track', split_axis=0, concat_axis=0, tiled=True)  6.72 us
  transfers between devices with their start and end apart: 20, of which 10 were waited for; matrix products, arithmetic and copies ran while one was open for 2% of the time, Pallas kernels for 30%

profile of v4, /device:TPU:1, one launch (start us, length us, event | category | flops | bytes accessed | tf_op | source)
XLA Modules:
  0.0 120.3 jit_solution(5918063739744610628)
XLA Ops:
  4.7 2.5 %collective-permute-start.2 = (f32[128,256]{1,0:T(8,128)S(1)}, f32[128,256]{1,0:T(8,128)S(1)}, u32[]{:S(2)}, u32[]{:S(2)}) collective-permute-start(f32[128,256]{1,0:T(8,128)S(1)} %maximum_multiply_fusion.refs_0_), channel_id=1, source_target_pairs={{0,2},{1,3},{2,4},{3,5},{4,6},{5,7},{6,8},{7,9},{8,10},{9,11},{10,... | collective-permute-start | bytes 393224 | tf_op jit(solution)/shard_map/ppermute | solution.py:272
  7.2 4.0 %collective-permute-start = (f32[128,256]{1,0:T(8,128)S(1)}, f32[128,256]{1,0:T(8,128)S(1)}, u32[]{:S(2)}, u32[]{:S(2)}) collective-permute-start(f32[128,256]{1,0:T(8,128)S(1)} %maximum_multiply_fusion.refs_0_), channel_id=1, source_target_pairs={{0,14},{1,15},{2,0},{3,1},{4,2},{5,3},{6,4},{7,5},{8,6},{9,7},{10,... | collective-permute-start | bytes 393224 | tf_op jit(solution)/shard_map/ppermute | solution.py:272
  11.3 6.7 %all-to-all-start = ((f32[16,17,128]{2,1,0:T(8,128)}), f32[16,17,128]{2,1,0:T(8,128)S(1)}, u32[]{:S(2)}, u32[]{:S(2)}) async-start(f32[16,17,128]{2,1,0:T(8,128)} %pad_maximum_fusion), calls=%async_computation | async-start | bytes 393216 | tf_op jit(solution)/shard_map/all_to_all | solution.py:307
  18.0 1.5 %collective-permute-start.3 = (f32[128,256]{1,0:T(8,128)S(1)}, f32[128,256]{1,0:T(8,128)S(1)}, u32[]{:S(2)}, u32[]{:S(2)}) collective-permute-start(f32[128,256]{1,0:T(8,128)S(1)} %collective-permute-done.2.refs_7_), channel_id=1, source_target_pairs={{0,2},{1,3},{2,4},{3,5},{4,6},{5,7},{6,8},{7,9},{8,10},{9,11},{10,... | collective-permute-start | bytes 393224 | tf_op jit(solution)/shard_map/ppermute | solution.py:272
  22.7 7.4 %shard_map.129.refs_0_ = bf16[2,2048,2048]{2,1,0:T(8,128)(2,1)} custom-call(s32[128]{0:T(128)S(1)} %bitcast.48, s32[128]{0:T(128)S(1)} %bitcast.50, s32[1]{0:T(128)} %bitcast.46.count_ref, f32[128,128,128]{2,1,0:T(8,128)} %bitcast.52), custom_call_target="tpu_custom_call" | custom-call | tf_op jit(solution)/shard_map/pallas_call | solution.py:98
  30.2 1.6 %broadcast_in_dim.2 = f32[16,16,8,256]{3,2,1,0:T(8,128)} broadcast(f32[16,8,256]{2,1,0:T(8,128)S(1)} %pad_maximum_fusion.1), dimensions={1,2,3} | broadcast | bytes 2228224 | tf_op jit(solution)/shard_map/broadcast_in_dim | solution.py:329
  31.8 8.4 %all-to-all-start.1 = ((f32[16,16,8,256]{3,2,1,0:T(8,128)}), f32[16,16,8,256]{3,2,1,0:T(8,128)S(1)}, u32[]{:S(2)}, u32[]{:S(2)}) async-start(f32[16,16,8,256]{3,2,1,0:T(8,128)} %broadcast_in_dim.2), calls=%async_computation.1 | async-start | bytes 4194304 | tf_op jit(solution)/shard_map/all_to_all | solution.py:328
  41.8 2.5 %collective-permute-done.4.refs_3_ = f32[128,256]{1,0:T(8,128)S(1)} collective-permute-done((f32[128,256]{1,0:T(8,128)S(1)}, f32[128,256]{1,0:T(8,128)S(1)}, u32[]{:S(2)}, u32[]{:S(2)}) %collective-permute-start.4) | collective-permute-done | bytes 131104 | tf_op jit(solution)/shard_map/ppermute | solution.py:272
  44.3 3.4 %collective-permute-start.5 = (f32[128,256]{1,0:T(8,128)S(1)}, f32[128,256]{1,0:T(8,128)S(1)}, u32[]{:S(2)}, u32[]{:S(2)}) collective-permute-start(f32[128,256]{1,0:T(8,128)S(1)} %collective-permute-done.4.refs_3_), channel_id=1, source_target_pairs={{0,14},{1,15},{2,0},{3,1},{4,2},{5,3},{6,4},{7,5},{8,6},{9,7},{10,... | collective-permute-start | bytes 393224 | tf_op jit(solution)/shard_map/ppermute | solution.py:272
  47.7 1.9 %collective-permute-done.5.refs_4_ = f32[128,256]{1,0:T(8,128)S(1)} collective-permute-done((f32[128,256]{1,0:T(8,128)S(1)}, f32[128,256]{1,0:T(8,128)S(1)}, u32[]{:S(2)}, u32[]{:S(2)}) %collective-permute-start.5) | collective-permute-done | bytes 131104 | tf_op jit(solution)/shard_map/ppermute | solution.py:272
  49.7 1.9 %collective-permute-start.7 = (f32[8,128,256]{2,1,0:T(8,128)S(1)}, f32[8,128,256]{2,1,0:T(8,128)S(1)}, u32[]{:S(2)}, u32[]{:S(2)}) collective-permute-start(f32[8,128,256]{2,1,0:T(8,128)S(1)} %shard_map.130.mine_ref), channel_id=1, source_target_pairs={{0,1},{1,0},{2,3},{3,2},{4,5},{5,4},{6,7},{7,6},{8,9},{9,8},{10,11... | collective-permute-start | bytes 3145736 | tf_op jit(solution)/shard_map/ppermute | solution.py:276
  51.6 7.4 %shard_map.131.adj_ref = bf16[2,2048,2048]{2,1,0:T(8,128)(2,1)} custom-call(s32[128]{0:T(128)S(1)} %bitcast.49, s32[128]{0:T(128)S(1)} %bitcast.51, s32[1]{0:T(128)} %bitcast.47.count_ref, f32[128,128,128]{2,1,0:T(8,128)} %bitcast.53, bf16[2,2048,2048]{2,1,0:T(8,128)(2,1)} %shard_map.129.refs_0_), custom_call_target="tpu_custom_call", output_to_operand_aliasing={{}: (4, {})} | custom-call | bytes 12582912 | tf_op jit(solution)/shard_map/pallas_call | solution.py:98
  59.1 11.3 %shard_map.132 = f32[2048,256]{1,0:T(8,128)} custom-call(f32[8,128,256]{2,1,0:T(8,128)S(1)} %shard_map.130.mine_ref, f32[8,128,256]{2,1,0:T(8,128)S(1)} %collective-permute-done.7.theirs_ref, bf16[2,2048,2048]{2,1,0:T(8,128)(2,1)} %shard_map.131.adj_ref), custom_call_target="tpu_custom_call" | custom-call | bytes 1048576 | tf_op jit(solution)/shard_map/pallas_call | solution.py:178
  70.7 8.0 %all-to-all-start.2 = ((f32[16,128,256]{2,1,0:T(8,128)}), f32[16,128,256]{2,1,0:T(8,128)}, u32[]{:S(2)}, u32[]{:S(2)}) async-start(f32[16,128,256]{2,1,0:T(8,128)} %bitcast.15), calls=%async_computation.2 | async-start | bytes 4194304 | tf_op jit(solution)/shard_map/all_to_all | solution.py:337
  78.7 9.7 %shard_map.133 = (f32[4,128,256]{2,1,0:T(8,128)S(1)}, f32[4,128,256]{2,1,0:T(8,128)S(1)}, f32[4,128,256]{2,1,0:T(8,128)S(1)}, f32[4,128,256]{2,1,0:T(8,128)S(1)}) custom-call(f32[16,16,8,256]{3,2,1,0:T(8,128)S(1)} %all-to-all-done.1.panel_ref, bf16[2,2048,2048]{2,1,0:T(8,128)(2,1)} %shard_map.131.adj_ref), custom_call_target="tpu_custom_call" | custom-call | bytes 1048576 | tf_op jit(solution)/shard_map/pallas_call | solution.py:237
  90.7 3.3 %collective-permute-start.11 = (f32[128,256]{1,0:T(8,128)S(1)}, f32[128,256]{1,0:T(8,128)S(1)}, u32[]{:S(2)}, u32[]{:S(2)}) collective-permute-start(f32[128,256]{1,0:T(8,128)S(1)} %get-tuple-element.41), channel_id=1, source_target_pairs={{0,14},{1,15},{2,0},{3,1},{4,2},{5,3},{6,4},{7,5},{8,6},{9,7},{10,... | collective-permute-start | bytes 393224 | tf_op jit(solution)/shard_map/ppermute | solution.py:272
  94.0 3.7 %collective-permute-done.10 = f32[128,256]{1,0:T(8,128)S(1)} collective-permute-done((f32[128,256]{1,0:T(8,128)S(1)}, f32[128,256]{1,0:T(8,128)S(1)}, u32[]{:S(2)}, u32[]{:S(2)}) %collective-permute-start.10) | collective-permute-done | bytes 131104 | tf_op jit(solution)/shard_map/ppermute | solution.py:272
  98.7 1.8 %collective-permute-start.13 = (f32[128,256]{1,0:T(8,128)S(1)}, f32[128,256]{1,0:T(8,128)S(1)}, u32[]{:S(2)}, u32[]{:S(2)}) collective-permute-start(f32[128,256]{1,0:T(8,128)S(1)} %get-tuple-element.43), channel_id=1, source_target_pairs={{0,14},{1,15},{2,0},{3,1},{4,2},{5,3},{6,4},{7,5},{8,6},{9,7},{10,... | collective-permute-start | bytes 393224 | tf_op jit(solution)/shard_map/ppermute | solution.py:272
  100.5 3.1 %collective-permute-done.12 = f32[128,256]{1,0:T(8,128)S(1)} collective-permute-done((f32[128,256]{1,0:T(8,128)S(1)}, f32[128,256]{1,0:T(8,128)S(1)}, u32[]{:S(2)}, u32[]{:S(2)}) %collective-permute-start.12) | collective-permute-done | bytes 131104 | tf_op jit(solution)/shard_map/ppermute | solution.py:272
  103.7 1.8 %collective-permute-start.14 = (f32[128,256]{1,0:T(8,128)S(1)}, f32[128,256]{1,0:T(8,128)S(1)}, u32[]{:S(2)}, u32[]{:S(2)}) collective-permute-start(f32[128,256]{1,0:T(8,128)S(1)} %get-tuple-element.44), channel_id=1, source_target_pairs={{0,2},{1,3},{2,4},{3,5},{4,6},{5,7},{6,8},{7,9},{8,10},{9,11},{10,... | collective-permute-start | bytes 393224 | tf_op jit(solution)/shard_map/ppermute | solution.py:272
  106.4 2.3 %collective-permute-done.14 = f32[128,256]{1,0:T(8,128)S(1)} collective-permute-done((f32[128,256]{1,0:T(8,128)S(1)}, f32[128,256]{1,0:T(8,128)S(1)}, u32[]{:S(2)}, u32[]{:S(2)}) %collective-permute-start.14) | collective-permute-done | bytes 131104 | tf_op jit(solution)/shard_map/ppermute | solution.py:272
  109.6 1.5 %all-to-all-done.2 = f32[16,128,256]{2,1,0:T(8,128)} async-done(((f32[16,128,256]{2,1,0:T(8,128)}), f32[16,128,256]{2,1,0:T(8,128)}, u32[]{:S(2)}, u32[]{:S(2)}) %all-to-all-start.2) | async-done | bytes 2097184 | tf_op jit(solution)/shard_map/all_to_all | solution.py:337
  112.2 1.7 %reduce_sum.11 = f32[128,256]{1,0:T(8,128)S(1)} reduce(f32[16,128,256]{2,1,0:T(8,128)} %all-to-all-done.2, f32[]{:T(128)} %constant.16.clone.1), dimensions={0}, to_apply=%region_0.0 | reduce | flops 491520 | bytes 2228228 | tf_op jit(solution)/shard_map/reduce_sum | solution.py:352
  114.6 4.9 %collective-permute-done.16 = f32[128,256]{1,0:T(8,128)S(1)} collective-permute-done((f32[128,256]{1,0:T(8,128)S(1)}, f32[128,256]{1,0:T(8,128)S(1)}, u32[]{:S(2)}, u32[]{:S(2)}) %collective-permute-start.16) | collective-permute-done | bytes 131104 | tf_op jit(solution)/shard_map/ppermute | solution.py:272
  (49 shorter events, 16.3 us)
Async XLA Ops:
  4.7 13.3 %collective-permute-start.2 = (f32[128,256]{1,0:T(8,128)S(1)}, f32[128,256]{1,0:T(8,128)S(1)}, u32[]{:S(2)}, u32[]{:S(2)}) collective-permute-start(f32[128,256]{1,0:T(8,128)S(1)} %maximum_multiply_fusion.refs_0_), channel_id=1, source_target_pairs={{0,2},{1,3},{2,4},{3,5},{4,6},{5,7},{6,8},{7,9},{8,10},{9,11},{10,... | collective-permute-start | bytes 393224 | tf_op jit(solution)/shard_map/ppermute | solution.py:272
  7.2 12.2 %collective-permute-start = (f32[128,256]{1,0:T(8,128)S(1)}, f32[128,256]{1,0:T(8,128)S(1)}, u32[]{:S(2)}, u32[]{:S(2)}) collective-permute-start(f32[128,256]{1,0:T(8,128)S(1)} %maximum_multiply_fusion.refs_0_), channel_id=1, source_target_pairs={{0,14},{1,15},{2,0},{3,1},{4,2},{5,3},{6,4},{7,5},{8,6},{9,7},{10,... | collective-permute-start | bytes 393224 | tf_op jit(solution)/shard_map/ppermute | solution.py:272
  11.3 18.9 %all-to-all-start = ((f32[16,17,128]{2,1,0:T(8,128)}), f32[16,17,128]{2,1,0:T(8,128)S(1)}, u32[]{:S(2)}, u32[]{:S(2)}) async-start(f32[16,17,128]{2,1,0:T(8,128)} %pad_maximum_fusion), calls=%async_computation | async-start | bytes 393216 | tf_op jit(solution)/shard_map/all_to_all | solution.py:307
  18.0 12.2 %collective-permute-start.3 = (f32[128,256]{1,0:T(8,128)S(1)}, f32[128,256]{1,0:T(8,128)S(1)}, u32[]{:S(2)}, u32[]{:S(2)}) collective-permute-start(f32[128,256]{1,0:T(8,128)S(1)} %collective-permute-done.2.refs_7_), channel_id=1, source_target_pairs={{0,2},{1,3},{2,4},{3,5},{4,6},{5,7},{6,8},{7,9},{8,10},{9,11},{10,... | collective-permute-start | bytes 393224 | tf_op jit(solution)/shard_map/ppermute | solution.py:272
  19.5 10.7 %collective-permute-start.1 = (f32[128,256]{1,0:T(8,128)S(1)}, f32[128,256]{1,0:T(8,128)S(1)}, u32[]{:S(2)}, u32[]{:S(2)}) collective-permute-start(f32[128,256]{1,0:T(8,128)S(1)} %collective-permute-done.refs_1_), channel_id=1, source_target_pairs={{0,14},{1,15},{2,0},{3,1},{4,2},{5,3},{6,4},{7,5},{8,6},{9,7},{10,... | collective-permute-start | bytes 393224 | tf_op jit(solution)/shard_map/ppermute | solution.py:272
  21.4 0.7 copy-start
  22.1 0.7 copy-start.2
  31.8 38.9 %all-to-all-start.1 = ((f32[16,16,8,256]{3,2,1,0:T(8,128)}), f32[16,16,8,256]{3,2,1,0:T(8,128)S(1)}, u32[]{:S(2)}, u32[]{:S(2)}) async-start(f32[16,16,8,256]{3,2,1,0:T(8,128)} %broadcast_in_dim.2), calls=%async_computation.1 | async-start | bytes 4194304 | tf_op jit(solution)/shard_map/all_to_all | solution.py:328
  40.2 11.4 %copy-start.1 = (s32[1,1,128]{2,1,0:T(1,128)S(1)}, s32[1,1,128]{2,1,0:T(1,128)}, u32[]{:S(2)}) copy-start(s32[1,1,128]{2,1,0:T(1,128)} %param.17) | copy-start | bytes 1540
  40.2 11.4 %copy-start.3 = (s32[1,1,128]{2,1,0:T(1,128)S(1)}, s32[1,1,128]{2,1,0:T(1,128)}, u32[]{:S(2)}) copy-start(s32[1,1,128]{2,1,0:T(1,128)} %param.18) | copy-start | bytes 1540
  40.2 4.1 %collective-permute-start.4 = (f32[128,256]{1,0:T(8,128)S(1)}, f32[128,256]{1,0:T(8,128)S(1)}, u32[]{:S(2)}, u32[]{:S(2)}) collective-permute-start(f32[128,256]{1,0:T(8,128)S(1)} %collective-permute-done.1.refs_2_), channel_id=1, source_target_pairs={{0,14},{1,15},{2,0},{3,1},{4,2},{5,3},{6,4},{7,5},{8,6},{9,7},{10,... | collective-permute-start | bytes 393224 | tf_op jit(solution)/shard_map/ppermute | solution.py:272
  41.5 6.2 %collective-permute-start.6 = (f32[128,256]{1,0:T(8,128)S(1)}, f32[128,256]{1,0:T(8,128)S(1)}, u32[]{:S(2)}, u32[]{:S(2)}) collective-permute-start(f32[128,256]{1,0:T(8,128)S(1)} %collective-permute-done.3.refs_6_), channel_id=1, source_target_pairs={{0,2},{1,3},{2,4},{3,5},{4,6},{5,7},{6,8},{7,9},{8,10},{9,11},{10,... | collective-permute-start | bytes 393224 | tf_op jit(solution)/shard_map/ppermute | solution.py:272
  44.3 5.4 %collective-permute-start.5 = (f32[128,256]{1,0:T(8,128)S(1)}, f32[128,256]{1,0:T(8,128)S(1)}, u32[]{:S(2)}, u32[]{:S(2)}) collective-permute-start(f32[128,256]{1,0:T(8,128)S(1)} %collective-permute-done.4.refs_3_), channel_id=1, source_target_pairs={{0,14},{1,15},{2,0},{3,1},{4,2},{5,3},{6,4},{7,5},{8,6},{9,7},{10,... | collective-permute-start | bytes 393224 | tf_op jit(solution)/shard_map/ppermute | solution.py:272
  49.7 9.3 %collective-permute-start.7 = (f32[8,128,256]{2,1,0:T(8,128)S(1)}, f32[8,128,256]{2,1,0:T(8,128)S(1)}, u32[]{:S(2)}, u32[]{:S(2)}) collective-permute-start(f32[8,128,256]{2,1,0:T(8,128)S(1)} %shard_map.130.mine_ref), channel_id=1, source_target_pairs={{0,1},{1,0},{2,3},{3,2},{4,5},{5,4},{6,7},{7,6},{8,9},{9,8},{10,11... | collective-permute-start | bytes 3145736 | tf_op jit(solution)/shard_map/ppermute | solution.py:276
  70.7 40.5 %all-to-all-start.2 = ((f32[16,128,256]{2,1,0:T(8,128)}), f32[16,128,256]{2,1,0:T(8,128)}, u32[]{:S(2)}, u32[]{:S(2)}) async-start(f32[16,128,256]{2,1,0:T(8,128)} %bitcast.15), calls=%async_computation.2 | async-start | bytes 4194304 | tf_op jit(solution)/shard_map/all_to_all | solution.py:337
  88.4 2.2 %collective-permute-start.9 = (f32[4,128,256]{2,1,0:T(8,128)S(1)}, f32[4,128,256]{2,1,0:T(8,128)S(1)}, u32[]{:S(2)}, u32[]{:S(2)}) collective-permute-start(f32[4,128,256]{2,1,0:T(8,128)S(1)} %get-tuple-element.39), channel_id=1, source_target_pairs={{0,1},{1,0},{2,3},{3,2},{4,5},{5,4},{6,7},{7,6},{8,9},{9,8},{10,11... | collective-permute-start | bytes 1572872 | tf_op jit(solution)/shard_map/ppermute | solution.py:276
  89.1 11.5 %collective-permute-start.8 = (f32[4,128,256]{2,1,0:T(8,128)S(1)}, f32[4,128,256]{2,1,0:T(8,128)S(1)}, u32[]{:S(2)}, u32[]{:S(2)}) collective-permute-start(f32[4,128,256]{2,1,0:T(8,128)S(1)} %get-tuple-element.37), channel_id=1, source_target_pairs={{0,1},{1,0},{2,3},{3,2},{4,5},{5,4},{6,7},{7,6},{8,9},{9,8},{10,11... | collective-permute-start | bytes 1572872 | tf_op jit(solution)/shard_map/ppermute | solution.py:276
  90.6 7.1 %collective-permute-start.10 = (f32[128,256]{1,0:T(8,128)S(1)}, f32[128,256]{1,0:T(8,128)S(1)}, u32[]{:S(2)}, u32[]{:S(2)}) collective-permute-start(f32[128,256]{1,0:T(8,128)S(1)} %get-tuple-element.40), channel_id=1, source_target_pairs={{0,2},{1,3},{2,4},{3,5},{4,6},{5,7},{6,8},{7,9},{8,10},{9,11},{10,... | collective-permute-start | bytes 393224 | tf_op jit(solution)/shard_map/ppermute | solution.py:272
  90.7 7.0 %collective-permute-start.11 = (f32[128,256]{1,0:T(8,128)S(1)}, f32[128,256]{1,0:T(8,128)S(1)}, u32[]{:S(2)}, u32[]{:S(2)}) collective-permute-start(f32[128,256]{1,0:T(8,128)S(1)} %get-tuple-element.41), channel_id=1, source_target_pairs={{0,14},{1,15},{2,0},{3,1},{4,2},{5,3},{6,4},{7,5},{8,6},{9,7},{10,... | collective-permute-start | bytes 393224 | tf_op jit(solution)/shard_map/ppermute | solution.py:272
  97.8 5.8 %collective-permute-start.12 = (f32[128,256]{1,0:T(8,128)S(1)}, f32[128,256]{1,0:T(8,128)S(1)}, u32[]{:S(2)}, u32[]{:S(2)}) collective-permute-start(f32[128,256]{1,0:T(8,128)S(1)} %get-tuple-element.42), channel_id=1, source_target_pairs={{0,2},{1,3},{2,4},{3,5},{4,6},{5,7},{6,8},{7,9},{8,10},{9,11},{10,... | collective-permute-start | bytes 393224 | tf_op jit(solution)/shard_map/ppermute | solution.py:272
  98.7 4.9 %collective-permute-start.13 = (f32[128,256]{1,0:T(8,128)S(1)}, f32[128,256]{1,0:T(8,128)S(1)}, u32[]{:S(2)}, u32[]{:S(2)}) collective-permute-start(f32[128,256]{1,0:T(8,128)S(1)} %get-tuple-element.43), channel_id=1, source_target_pairs={{0,14},{1,15},{2,0},{3,1},{4,2},{5,3},{6,4},{7,5},{8,6},{9,7},{10,... | collective-permute-start | bytes 393224 | tf_op jit(solution)/shard_map/ppermute | solution.py:272
  103.7 5.1 %collective-permute-start.14 = (f32[128,256]{1,0:T(8,128)S(1)}, f32[128,256]{1,0:T(8,128)S(1)}, u32[]{:S(2)}, u32[]{:S(2)}) collective-permute-start(f32[128,256]{1,0:T(8,128)S(1)} %get-tuple-element.44), channel_id=1, source_target_pairs={{0,2},{1,3},{2,4},{3,5},{4,6},{5,7},{6,8},{7,9},{8,10},{9,11},{10,... | collective-permute-start | bytes 393224 | tf_op jit(solution)/shard_map/ppermute | solution.py:272
  105.5 4.1 %collective-permute-start.15 = (f32[128,256]{1,0:T(8,128)S(1)}, f32[128,256]{1,0:T(8,128)S(1)}, u32[]{:S(2)}, u32[]{:S(2)}) collective-permute-start(f32[128,256]{1,0:T(8,128)S(1)} %get-tuple-element.45), channel_id=1, source_target_pairs={{0,14},{1,15},{2,0},{3,1},{4,2},{5,3},{6,4},{7,5},{8,6},{9,7},{10,... | collective-permute-start | bytes 393224 | tf_op jit(solution)/shard_map/ppermute | solution.py:272
  111.2 8.4 %collective-permute-start.16 = (f32[128,256]{1,0:T(8,128)S(1)}, f32[128,256]{1,0:T(8,128)S(1)}, u32[]{:S(2)}, u32[]{:S(2)}) collective-permute-start(f32[128,256]{1,0:T(8,128)S(1)} %fusion.1), channel_id=1, source_target_pairs={{0,2},{1,3},{2,4},{3,5},{4,6},{5,7},{6,8},{7,9},{8,10},{9,11},{10,... | collective-permute-start | bytes 393224 | tf_op jit(solution)/shard_map/ppermute | solution.py:272
